TPU v7x, 512 devices: a whole 4x4x16 slice. The times are simulated.
512 devices in a mesh: frame: 64 (over z, x_lo, core), row: 8 (over y, x_hi).
Axes of the slice: x: 4 (x_hi: 2, x_lo: 2; x = x_hi * 2 + x_lo), y: 4, z: 16, core: 2. Of those that a mesh axis runs over, the one named last changes fastest.
Arguments:
- video: bfloat16 [64, 32, 32, 3072], P('frame', 'row'), may hold values from -18 to 18
- qkv_weight: bfloat16 [3072, 3, 2048], P('frame', None, 'row'), may hold values from -1 to 1
- window: int32 [16, 3], P('row'), may hold values from 0 to 1, as said below
- clips: int32 [64], replicated, may hold values from 0 to 15, never falling along the last dimension, each value on 1 to 8 neighbouring positions
Outputs:
- attended: bfloat16 [64, 32, 32, 2048], P('frame', None, None, 'row')
Inputs may be any that keep to these rules, and one draw needn't show every extreme that they name: window[h, 0], window[h, 1] and window[h, 2] are head h's reaches along frames, row tiles and column tiles; in every group of 2 consecutive heads along each of the three, some head has reach 1. `clips`: clip numbers never fall along the frames; each clip has 1 to 8 frames.
All inputs are finite; a program needn't handle non-finite values.
Results may differ from a plain program's by a relative error of at most 0.0068.
Values may be sent and summed in bfloat16 or wider, within the bound.
No kernel may reach another device: no remote copies, remote signals or barrier semaphores. Data moves between devices by JAX's collectives and lax.ppermute only.
A program may use at most 64 MiB of HBM per device.

v0:
```python
import math

import jax
import jax.numpy as jnp
from jax import lax
from jax.sharding import PartitionSpec as P

HD = 128
TH = 8
TW = 8


def with_halo(value, sides, width):
    for axis, dim in sides:
        count, length = (lax.axis_size(axis), value.shape[dim])
        up = [(i, (i + 1) % count) for i in range(count - 1)]
        down = [(j, i) for i, j in up]
        last = lax.slice_in_dim(value, length - width, length, axis=dim)
        initial = lax.slice_in_dim(value, 0, width, axis=dim)
        before = lax.ppermute(last, axis, up)
        after = lax.ppermute(initial, axis, down)
        value = jnp.concatenate([before, value, after], axis=dim)
    return value


def body(video, qkv_weight, window, clips):
    frame_here = lax.axis_index("frame")
    local_width = qkv_weight.shape[2]
    head_count = local_width // HD
    features = video.shape[3]
    qkv_matrix = lax.all_gather(qkv_weight, "frame", axis=0, tiled=True).reshape(
        features, 3 * local_width
    )
    shard_rows = lax.all_gather(video, "row", axis=1, tiled=True)
    flattened = shard_rows.reshape(-1, features)
    result = jnp.dot(flattened, qkv_matrix, preferred_element_type=jnp.float32).astype(jnp.bfloat16)
    projected = result.reshape(
        shard_rows.shape[0], shard_rows.shape[1], shard_rows.shape[2], 3 * local_width
    )
    row_count = projected.shape[1]
    col_count = projected.shape[2]
    tokens = row_count * col_count
    projected = projected.reshape(tokens, 3 * local_width)
    queries = projected[:, :local_width]
    keyval = projected[:, local_width:].reshape(1, tokens, 2 * local_width)
    nearby = with_halo(keyval, (("frame", 0),), 1)
    edge_clip = jnp.full((1,), -1, jnp.int32)
    padded_clips = jnp.concatenate([edge_clip, clips, edge_clip])
    nearby_clips = lax.dynamic_slice_in_dim(padded_clips, frame_here, 3, 0)
    same_clip = nearby_clips == nearby_clips[1]
    frame_gap = jnp.abs(jnp.arange(3) - 1)
    frame_allowed = (frame_gap[None, :] <= window[:, 0:1]) & same_clip[None, :]
    tile_count = row_count // TH
    block_tiles = tile_count
    while block_tiles % 2 == 0 and block_tiles * TH * col_count > 512:
        block_tiles = block_tiles // 2
    band_tiles = min(tile_count, block_tiles + 2)
    positions = jnp.arange(tokens)
    tile_row = positions // col_count // TH
    tile_column = positions % col_count // TW
    score_scale = 1.0 / math.sqrt(HD)
    outputs = []
    for block_index in range(tile_count // block_tiles):
        first_tile = block_index * block_tiles
        band_start = min(max(first_tile - 1, 0), tile_count - band_tiles)
        query_from = first_tile * TH * col_count
        query_count = block_tiles * TH * col_count
        key_from = band_start * TH * col_count
        key_count = band_tiles * TH * col_count
        row_gap = jnp.abs(
            tile_row[query_from : query_from + query_count, None]
            - tile_row[None, key_from : key_from + key_count]
        )
        column_gap = jnp.abs(
            tile_column[query_from : query_from + query_count, None]
            - tile_column[None, key_from : key_from + key_count]
        )
        head_blocks = []
        for head_index in range(head_count):
            low = head_index * HD
            query_head = queries[query_from : query_from + query_count, low : low + HD]
            key_head = nearby[:, :, low : low + HD].reshape(3 * key_count, HD)
            value_head = nearby[:, :, local_width + low : local_width + low + HD].reshape(
                3 * key_count, HD
            )
            scores = (
                lax.dot_general(
                    query_head,
                    key_head,
                    (((1,), (1,)), ((), ())),
                    preferred_element_type=jnp.float32,
                )
                * score_scale
            )
            inside = (row_gap <= window[head_index, 1]) & (column_gap <= window[head_index, 2])
            allowed = (frame_allowed[head_index][None, :, None] & inside[:, None, :]).reshape(
                query_count, 3 * key_count
            )
            masked = jnp.where(allowed, scores, -1e30)
            row_max = jnp.max(masked, axis=1, keepdims=True)
            weight = jnp.exp(masked - row_max)
            totals = jnp.sum(weight, axis=1, keepdims=True)
            blended = (
                jnp.dot(weight.astype(jnp.bfloat16), value_head, preferred_element_type=jnp.float32)
                / totals
            )
            head_blocks.append(blended.astype(jnp.bfloat16))
        outputs.append(jnp.concatenate(head_blocks, axis=1))
    attended = jnp.concatenate(outputs, axis=0)
    return attended.reshape(1, row_count, col_count, local_width)


def solution(mesh):
    placed = (P("frame", "row", None, None), P("frame", None, "row"), P("row", None), P())
    return jax.shard_map(
        body, mesh=mesh, in_specs=placed, out_specs=P("frame", None, None, "row"), check_vma=False
    )
```

profile of v0, /device:TPU:6, one launch (start us, length us, event | category | flops | bytes accessed | tf_op | source)
XLA Modules:
  0.0 306.9 jit_solution(17706026127067027402)
XLA Ops:
  6.5 0.7 all-gather.5.cloned.1.call-update
  8.0 1.5 fusion.80
  9.5 129.7 %all-gather.5.cloned.1.call-done = bf16[3072,3,256]{2,0,1:T(8,128)(2,1)} async-done(((bf16[48,3,256]{2,0,1:T(8,128)(2,1)}), bf16[3072,3,256]{2,0,1:T(8,128)(2,1)}) %all-gather.5.cloned.1.call-update) | async-done | bytes 4718608 | tf_op jit(solution)/shard_map/all_gather | solution.py:31
  139.2 6.7 %copy.14 = bf16[3072,3,256]{0,2,1:T(8,128)(2,1)} copy(bf16[3072,3,256]{2,0,1:T(8,128)(2,1)} %all-gather.5.cloned.1.call-done) | data formatting | bytes 9437184 | tf_op jit(solution)/shard_map/all_gather | solution.py:31
  145.9 95.8 %all-gather.3.cloned.1.call-done = bf16[1,32,32,3072]{3,2,0,1:T(8,128)(2,1)} async-done(((bf16[1,4,32,3072]{3,2,0,1:T(8,128)(2,1)}), bf16[1,32,32,3072]{3,2,0,1:T(8,128)(2,1)}) %all-gather.3.cloned.1.call-update) | async-done | bytes 6291472 | tf_op jit(solution)/shard_map/all_gather | solution.py:34
  241.7 8.6 %convolution_convert_fusion = bf16[1024,768]{1,0:T(8,128)(2,1)S(1)} fusion(bf16[1024,3072]{1,0:T(8,128)(2,1)} %bitcast.47, bf16[3072,768]{0,1:T(8,128)(2,1)} %bitcast.45), kind=kOutput, calls=%fused_computation.41 | convolution fusion | flops 4832624640 | bytes 12582912 | tf_op jit(solution)/shard_map/dot_general | solution.py:36
  250.3 1.1 slice_bitcast_fusion
  251.5 1.9 collective-permute-start.1
  253.4 2.4 collective-permute-start
  255.8 6.5 %fusion.28 = (pred[512,1024]{0,1:T(8,128)(4,1)}, pred[512,1024]{0,1:T(8,128)(4,1)}, pred[512,1024]{0,1:T(8,128)(4,1)S(1)}, pred[512,1024]{0,1:T(8,128)(4,1)S(1)}) fusion(s32[]{:T(128)} %bitcast.3, s32[1024]{0:T(1024)S(1)} %get-tuple-element.33, s32[512]{0:T(512)S(1)} %get-tuple-element.17, s32[]{:T(128)} %bitcast.2, s32[1024]{0:T(1024)S(1)} %get-tuple-element.34, ...), kind=kLoop, calls=%fused_computation.37 | loop fusion | flops 10485760 | bytes 2113552 | tf_op jit(solution)/shard_map/and | solution.py:95
  262.7 1.7 copy.17
  265.2 0.7 broadcast_compare_fusion
  266.7 1.7 copy.16
  268.5 1.5 and.202
  270.0 1.7 copy.15
  272.1 1.7 copy.12
  273.8 5.8 %collective-permute-done = bf16[1,1024,512]{2,1,0:T(8,128)(2,1)} collective-permute-done((bf16[1,1024,512]{2,1,0:T(8,128)(2,1)}, bf16[1,1024,512]{2,1,0:T(8,128)(2,1)}, u32[]{:S(2)}, u32[]{:S(2)}) %collective-permute-start) | collective-permute-done | bytes 1048608 | tf_op jit(solution)/shard_map/ppermute | solution.py:20
  279.6 2.2 pad_maximum_fusion
  282.4 0.8 copy-done.1
  283.2 1.6 fusion.81
  284.9 1.9 fusion.83
  286.7 1.0 fusion.6
  287.7 1.3 fusion.53
  289.0 1.0 fusion.2
  290.0 1.3 fusion.41
  291.2 1.6 fusion.82
  292.9 1.6 fusion.84
  294.5 1.0 fusion.4
  295.5 1.3 fusion.47
  296.8 1.0 fusion
  297.8 1.3 fusion.35
  299.1 1.0 copy.18
  (32 shorter events, 3.8 us)
Async XLA Ops:
  6.5 132.7 %all-gather.5.cloned.1.call-start = ((), (), s32[]{:S(2)}) async-start(), calls=%async_computation.1 | async-start | bytes 4792320 | tf_op jit(solution)/shard_map/all_gather | solution.py:31
  7.3 234.5 %all-gather.3.cloned.1.call-start = ((), (), s32[]{:S(2)}) async-start(), calls=%async_computation | async-start | bytes 7077888 | tf_op jit(solution)/shard_map/all_gather | solution.py:34
  250.3 12.4 %copy-start = (bf16[1024,768]{1,0:T(8,128)(2,1)}, bf16[1024,768]{1,0:T(8,128)(2,1)S(1)}, u32[]{:S(2)}) copy-start(bf16[1024,768]{1,0:T(8,128)(2,1)S(1)} %convolution_convert_fusion) | copy-start | bytes 4718596
  251.5 22.4 %collective-permute-start.1 = (bf16[1,1024,512]{2,1,0:T(8,128)(2,1)}, bf16[1,1024,512]{2,1,0:T(8,128)(2,1)}, u32[]{:S(2)}, u32[]{:S(2)}) collective-permute-start(bf16[1,1024,512]{2,1,0:T(8,128)(2,1)} %slice_bitcast_fusion), channel_id=1, source_target_pairs={{8,0},{16,8},{24,16},{32,24},{40,32},{48,40},{56,48},{64,56},{72,6... | collective-permute-start | bytes 3145736 | tf_op jit(solution)/shard_map/ppermute | solution.py:21
  253.4 26.3 %collective-permute-start = (bf16[1,1024,512]{2,1,0:T(8,128)(2,1)}, bf16[1,1024,512]{2,1,0:T(8,128)(2,1)}, u32[]{:S(2)}, u32[]{:S(2)}) collective-permute-start(bf16[1,1024,512]{2,1,0:T(8,128)(2,1)} %slice_bitcast_fusion), channel_id=1, source_target_pairs={{0,8},{8,16},{16,24},{24,32},{32,40},{40,48},{48,56},{56,64},{64,7... | collective-permute-start | bytes 3145736 | tf_op jit(solution)/shard_map/ppermute | solution.py:20
  262.3 2.1 copy-start.4
  262.3 3.6 %copy-start.3 = (s32[2,3]{1,0:T(2,128)S(1)}, s32[2,3]{1,0:T(2,128)}, u32[]{:S(2)}) copy-start(s32[2,3]{1,0:T(2,128)} %param.6) | copy-start | bytes 76
  268.5 3.2 %copy-start.2 = (pred[512,1024]{0,1:T(8,128)(4,1)S(1)}, pred[512,1024]{0,1:T(8,128)(4,1)}, u32[]{:S(2)}) copy-start(pred[512,1024]{0,1:T(8,128)(4,1)} %get-tuple-element.9) | copy-start | bytes 1572868
  281.8 1.4 copy-start.1
Sparse Core Ops, SparseCore 0:
  9.5 129.7 all-gather.4
  142.4 99.2 all-gather.2
where the time goes:
time: 309 us; the launch traced here: 307 us
  waiting for transfers between devices  233 us (75%)
  local copies, waits for them, and re-layouts  22.2 us (7%)
  matrix products  20.4 us (7%)
  other arithmetic  13.6 us (4%)
  between operations  13.6 us (4%)
  starting transfers between devices  4.36 us (1%)
    all_gather x1, waiting for transfers between devices, body(): lax.all_gather(qkv_weight, 'frame', axis=0, tiled=True)  130 us
    all_gather x1, waiting for transfers between devices, body(): shard_rows = lax.all_gather(video, 'row', axis=1, tiled=True)  95.8 us
    and x13, local copies, waits for them, and re-layouts, body(): frame_allowed[head_index][None, :, None] & inside[:, None, :]  9.75 us
    dot_general x1, matrix products, body(): jnp.dot(flattened, qkv_matrix, preferred_element_type=jnp.float32)  8.6 us
    dot_general x4, matrix products, body(): lax.dot_general(query_head, key_head, (((1,), (1,)), ((), ())), preferred...  6.74 us
    all_gather x1, local copies, waits for them, and re-layouts, body(): lax.all_gather(qkv_weight, 'frame', axis=0, tiled=True)  6.67 us
    and x1, other arithmetic, body(): (row_gap <= window[head_index, 1]) & (column_gap <= window[head_index, 2])  6.53 us
  transfers between devices with their start and end apart: 4, of which 3 were waited for; matrix products, arithmetic and copies ran while one was open for 9% of the time, Pallas kernels for 0%

commit v1 on v0

v1 whole, which is shorter than its diff:
```python
import functools
import math

import jax
import jax.numpy as jnp
from jax import lax
from jax.experimental import pallas as pl
from jax.experimental.pallas import tpu as pltpu
from jax.sharding import PartitionSpec as P

HD = 128
TH = 8
TW = 8
COLS = 32
TILE = TH * COLS
NEG = -1e30
SCALE = math.log2(math.e) / math.sqrt(HD)
GROUP = 4


def key_marks(tile, reach_row, reach_col, bias):
    lane = lax.broadcasted_iota(jnp.int32, (TILE, HD), 1)
    col = (lax.broadcasted_iota(jnp.int32, (TILE, HD), 0) % COLS) // TW
    by_col = jnp.where(jnp.abs(lane - col) <= reach_col, 0.0, NEG)
    by_row = jnp.where(jnp.abs(lane - 4 - tile) <= reach_row, 0.0, NEG)
    marks = jnp.where(lane < 4, by_col, jnp.where(lane < 8, by_row, jnp.where(lane == 8, bias, 0.0)))
    return marks.astype(jnp.bfloat16)


def query_marks(tile):
    lane = lax.broadcasted_iota(jnp.int32, (TILE, HD), 1)
    col = (lax.broadcasted_iota(jnp.int32, (TILE, HD), 0) % COLS) // TW
    hot = (lane == col) | (lane == 4 + tile) | (lane == 8)
    return hot.astype(jnp.float32).astype(jnp.bfloat16)


def attend_kernel(frames, first, final, tiles, *refs):
    flags, q = refs[0], refs[1]
    kvs = refs[2 : 2 + frames]
    rest = refs[2 + frames :]
    if not first:
        acc_in, top_in = rest[0], rest[1]
        rest = rest[2:]
    ones = jnp.ones((TILE, HD), jnp.bfloat16)
    marks = [query_marks(t) for t in range(tiles)]
    for h in range(2):
        keys, values = [], []
        for i in range(frames):
            bias = jnp.where(flags[6 + 2 * i + h] != 0, 0.0, NEG)
            for t in range(tiles):
                rows = pl.ds(t * TILE, TILE)
                key = kvs[i][rows, h * HD : (h + 1) * HD]
                value = kvs[i][rows, (2 + h) * HD : (3 + h) * HD]
                mark = key_marks(t, flags[h * 3 + 1], flags[h * 3 + 2], bias)
                keys.append(jnp.concatenate([key, mark], axis=1))
                values.append(jnp.concatenate([value, ones], axis=1))
        for t in range(tiles):
            rows = pl.ds(t * TILE, TILE)
            query = jnp.concatenate([q[rows, h * HD : (h + 1) * HD], marks[t]], axis=1)
            near = [i * tiles + u for i in range(frames) for u in range(max(t - 1, 0), min(t + 2, tiles))]
            scores = [
                lax.dot_general(
                    query, keys[j], (((1,), (1,)), ((), ())), preferred_element_type=jnp.float32
                )
                for j in near
            ]
            top = functools.reduce(jnp.maximum, scores)
            top = jnp.max(top, axis=1, keepdims=True)
            if not first:
                old = top_in[rows, h : h + 1]
                top = jnp.maximum(top, old)
            shift = top * SCALE
            weight = jnp.concatenate(
                [jnp.exp2(s * SCALE - shift).astype(jnp.bfloat16) for s in scores], axis=1
            )
            value = jnp.concatenate([values[j] for j in near], axis=0)
            acc = jnp.dot(weight, value, preferred_element_type=jnp.float32)
            wide = slice(2 * h * HD, 2 * (h + 1) * HD)
            if not first:
                acc = acc + acc_in[rows, wide] * jnp.exp2(old * SCALE - shift)
            if final:
                rest[0][rows, h * HD : (h + 1) * HD] = (acc[:, :HD] / acc[:, HD:]).astype(jnp.bfloat16)
            else:
                rest[0][rows, wide] = acc
                rest[1][rows, h : h + 1] = top


def attend(flags, q, kvs, state=None, final=True):
    tokens = q.shape[0]
    frames = len(kvs)
    vmem = pl.BlockSpec(memory_space=pltpu.VMEM)
    arrays = [q, *kvs, *(state or ())]
    if final:
        out = jax.ShapeDtypeStruct((tokens, 2 * HD), jnp.bfloat16)
    else:
        out = (
            jax.ShapeDtypeStruct((tokens, 4 * HD), jnp.float32),
            jax.ShapeDtypeStruct((tokens, HD), jnp.float32),
        )
    pairs = frames * 2 * 10 * TILE * TILE
    return pl.pallas_call(
        functools.partial(attend_kernel, frames, state is None, final, tokens // TILE),
        out_shape=out,
        in_specs=[pl.BlockSpec(memory_space=pltpu.SMEM)] + [vmem] * len(arrays),
        out_specs=vmem if final else (vmem, vmem),
        compiler_params=pltpu.CompilerParams(vmem_limit_bytes=48 * 1024 * 1024),
        cost_estimate=pl.CostEstimate(
            flops=pairs * 1024, bytes_accessed=(frames + 3) << 20, transcendentals=pairs
        ),
    )(flags, *arrays)


def body(video, qkv_weight, window, clips):
    frame_here = lax.axis_index("frame")
    frames = lax.axis_size("frame")
    width = qkv_weight.shape[2]
    features = video.shape[3]
    rows = video.shape[1] * lax.axis_size("row")

    shard = qkv_weight.reshape(-1, 3 * width)
    near = [[g * GROUP + i for i in range(GROUP)] for g in range(frames // GROUP)]
    far = [[g * GROUP + i for g in range(frames // GROUP)] for i in range(GROUP)]
    shard = lax.all_gather(shard, "frame", axis=0, tiled=True, axis_index_groups=near)
    matrix = lax.all_gather(shard, "frame", axis=0, tiled=True, axis_index_groups=far)

    block, shard = lax.optimization_barrier((video.reshape(1, -1, features), shard))
    copies = jnp.broadcast_to(block, (lax.axis_size("row"), *block.shape[1:]))
    tokens = lax.all_to_all(copies, "row", 0, 0).reshape(-1, features)

    kv = jnp.dot(tokens, matrix[:, width:], preferred_element_type=jnp.float32).astype(jnp.bfloat16)
    up = [(i, i + 1) for i in range(frames - 1)]
    before = lax.ppermute(kv, "frame", up)
    after = lax.ppermute(kv, "frame", [(j, i) for i, j in up])
    q = jnp.dot(tokens, matrix[:, :width], preferred_element_type=jnp.float32).astype(jnp.bfloat16)

    edge = jnp.full((1,), -1, jnp.int32)
    near_clips = lax.dynamic_slice_in_dim(jnp.concatenate([edge, clips, edge]), frame_here, 3, 0)
    reach = window[:, 0]
    flag = lambda side: ((reach >= 1) & (near_clips[side] == near_clips[1])).astype(jnp.int32)
    head = window.reshape(-1)
    here = jnp.concatenate([head, jnp.ones((2,), jnp.int32)])
    sides = jnp.concatenate([head, flag(0), flag(2)])

    state = attend(here, q, [kv], None, False)
    out = attend(sides, q, [before, after], state, True)
    return out.reshape(1, rows, -1, width)


def solution(mesh):
    placed = (P("frame", "row", None, None), P("frame", None, "row"), P("row", None), P())
    return jax.shard_map(
        body, mesh=mesh, in_specs=placed, out_specs=P("frame", None, None, "row"), check_vma=False
    )
```

time: 309 us -> 150 us (0.49)
  waiting for transfers between devices: 233 us -> 81.8 us
  local copies, waits for them, and re-layouts: 22.2 us -> 6.28 us
  other arithmetic: 13.6 us -> 0.3 us
  starting transfers between devices: 4.36 us -> 16.2 us
  Pallas kernels: 0 us -> 9.07 us
  matrix products: 20.4 us -> 12.1 us
  blocking collectives: 0 us -> 6.31 us
    all_gather x2 -> x1, waiting for transfers between devices: 226 us -> 0.01 us  [body(): lax.all_gather(shard, 'frame', axis=0, tiled=True, axis_index_groups=far)]
    all_to_all x0 -> x1, waiting for transfers between devices: none -> 71.5 us  [body(): tokens = lax.all_to_all(copies, 'row', 0, 0).reshape(-1, features)]
    all_to_all x0 -> x1, starting transfers between devices: none -> 10.6 us  [body(): tokens = lax.all_to_all(copies, 'row', 0, 0).reshape(-1, features)]
    and x13 -> x0, local copies, waits for them, and re-layouts: 9.75 us -> none  [body(): frame_allowed[head_index][None, :, None] & inside[:, None, :]]
    pallas_call x0 -> x2, Pallas kernels: none -> 9.07 us  [attend(): pl.pallas_call(functools.partial(attend_kernel, frames, state is None, fi...]
    dot_general x9 -> x2, matrix products: 20.4 us -> 12.1 us  [the longest x1 7.12 us: body(): jnp.dot(tokens, matrix[:, width:], preferred_element_type=jnp.float32)]
    all_gather x1 -> x0, local copies, waits for them, and re-layouts: 6.67 us -> none  [body(): lax.all_gather(qkv_weight, 'frame', axis=0, tiled=True)]
    and x2 -> x0, other arithmetic: 6.6 us -> none  [the longest x1 6.53 us: body(): (row_gap <= window[head_index, 1]) & (column_gap <= window[head_index, 2])]
  transfers between devices with their start and end apart: 4 -> 4, of which waited for: 3 -> 2; matrix products, arithmetic and copies ran while one was open for 9% -> 7% of each run, Pallas kernels for 0% -> 2%
where the time goes in v1:
time: 150 us; the launch traced here: 148 us
  waiting for transfers between devices  81.8 us (55%)
  starting transfers between devices  16.2 us (11%)
  between operations  15.9 us (11%)
  matrix products  12.1 us (8%)
  Pallas kernels  9.07 us (6%)
  blocking collectives  6.31 us (4%)
  local copies, waits for them, and re-layouts  6.28 us (4%)
    all_to_all x1, waiting for transfers between devices, body(): tokens = lax.all_to_all(copies, 'row', 0, 0).reshape(-1, features)  71.5 us
    all_to_all x1, starting transfers between devices, body(): tokens = lax.all_to_all(copies, 'row', 0, 0).reshape(-1, features)  10.6 us
    ppermute x1, waiting for transfers between devices, body(): before = lax.ppermute(kv, 'frame', up)  10.3 us
    pallas_call x2, Pallas kernels, attend(): pl.pallas_call(functools.partial(attend_kernel, frames, state is None, fi...  9.07 us
    dot_general x1, matrix products, body(): jnp.dot(tokens, matrix[:, width:], preferred_element_type=jnp.float32)  7.12 us
    all_gather x1, blocking collectives, body(): lax.all_gather(shard, 'frame', axis=0, tiled=True, axis_index_groups=near)  6.31 us
    dot_general x1, matrix products, body(): jnp.dot(tokens, matrix[:, :width], preferred_element_type=jnp.float32)  5.02 us
    broadcast_in_dim x1, local copies, waits for them, and re-layouts, body(): copies = jnp.broadcast_to(block, (lax.axis_size('row'), *block.shape[1:]))  4.62 us
  transfers between devices with their start and end apart: 4, of which 2 were waited for; matrix products, arithmetic and copies ran while one was open for 7% of the time, Pallas kernels for 2%

profile of v1, /device:TPU:6, one launch (start us, length us, event | category | flops | bytes accessed | tf_op | source)
XLA Modules:
  0.0 148.0 jit_solution(11524832545163212867)
XLA Ops:
  6.5 0.0 all-gather.2.cloned.1.call-start
  6.5 0.9 copy.6
  7.4 6.3 %all_gather.6 = bf16[192,768]{1,0:T(8,128)(2,1)} all-gather(bf16[48,768]{1,0:T(8,128)(2,1)S(1)} %bitcast.11), channel_id=1, replica_groups={{0,8,16,24},{32,40,48,56},{64,72,80,88},{96,104,112,120},{128,136,144,1..., dimensions={0}, use_global_device_ids=true | all-gather | bytes 368640 | tf_op jit(solution)/shard_map/all_gather | solution.py:123
  13.7 0.0 all-gather.2.cloned.1.call-update
  13.8 4.6 %broadcast_in_dim.8 = bf16[8,128,3072]{2,1,0:T(8,128)(2,1)} broadcast(bf16[128,3072]{1,0:T(8,128)(2,1)} %bitcast.10), dimensions={1,2} | broadcast | bytes 7077888 | tf_op jit(solution)/shard_map/broadcast_in_dim | solution.py:127
  18.4 0.0 copy-start.1
  18.4 10.6 %all-to-all-start = ((bf16[8,128,3072]{2,1,0:T(8,128)(2,1)}), bf16[8,128,3072]{2,1,0:T(8,128)(2,1)}, u32[]{:S(2)}, u32[]{:S(2)}) async-start(bf16[8,128,3072]{2,1,0:T(8,128)(2,1)} %broadcast_in_dim.8), calls=%async_computation | async-start | bytes 12582912 | tf_op jit(solution)/shard_map/all_to_all | solution.py:128
  29.0 0.0 copy-done.1
  29.0 0.1 pad_add_fusion
  29.1 0.1 dynamic_slice.3
  29.2 71.5 %all-to-all-done = bf16[8,128,3072]{2,1,0:T(8,128)(2,1)} async-done(((bf16[8,128,3072]{2,1,0:T(8,128)(2,1)}), bf16[8,128,3072]{2,1,0:T(8,128)(2,1)}, u32[]{:S(2)}, u32[]{:S(2)}) %all-to-all-start) | async-done | bytes 6291488 | tf_op jit(solution)/shard_map/all_to_all | solution.py:128
  100.6 0.0 all-gather.2.cloned.1.call-done
  100.7 0.0 copy-start
  100.7 7.1 %fusion.4.refs_2_ = bf16[1024,512]{1,0:T(8,128)(2,1)S(1)} fusion(bf16[1024,3072]{1,0:T(8,128)(2,1)} %bitcast.4, bf16[3072,768]{1,0:T(8,128)(2,1)} %all-gather.2.cloned.1.call-done), kind=kOutput, calls=%fused_computation.4 | convolution fusion | flops 3221749760 | bytes 10485760 | tf_op jit(solution)/shard_map/dot_general | solution.py:130
  107.8 1.9 %collective-permute-start = (bf16[1024,512]{1,0:T(8,128)(2,1)S(1)}, bf16[1024,512]{1,0:T(8,128)(2,1)S(1)}, u32[]{:S(2)}, u32[]{:S(2)}) collective-permute-start(bf16[1024,512]{1,0:T(8,128)(2,1)S(1)} %fusion.4.refs_2_), channel_id=1, source_target_pairs={{0,8},{8,16},{16,24},{24,32},{32,40},{40,48},{48,56},{56,64},{64,7... | collective-permute-start | bytes 3145736 | tf_op jit(solution)/shard_map/ppermute | solution.py:132
  109.7 3.6 %collective-permute-start.1 = (bf16[1024,512]{1,0:T(8,128)(2,1)S(1)}, bf16[1024,512]{1,0:T(8,128)(2,1)S(1)}, u32[]{:S(2)}, u32[]{:S(2)}) collective-permute-start(bf16[1024,512]{1,0:T(8,128)(2,1)S(1)} %fusion.4.refs_2_), channel_id=1, source_target_pairs={{8,0},{16,8},{24,16},{32,24},{40,32},{48,40},{56,48},{64,56},{72,6... | collective-permute-start | bytes 3145736 | tf_op jit(solution)/shard_map/ppermute | solution.py:133
  113.4 0.6 fusion.12
  116.4 0.0 copy-done
  116.4 0.1 reshape.27
  116.5 0.1 fusion.10
  116.7 0.1 pad_add_fusion.1.refs_0_
  116.8 5.0 %fusion.7.refs_1_ = bf16[1024,256]{1,0:T(8,128)(2,1)S(1)} fusion(bf16[1024,3072]{1,0:T(8,128)(2,1)} %bitcast.4, bf16[3072,768]{1,0:T(8,128)(2,1)} %all-gather.2.cloned.1.call-done), kind=kOutput, calls=%fused_computation.5 | convolution fusion | flops 1610874880 | bytes 8388608 | tf_op jit(solution)/shard_map/dot_general | solution.py:134
  121.8 3.1 %shard_map.46 = (f32[1024,512]{1,0:T(8,128)S(1)}, f32[1024,128]{1,0:T(8,128)S(1)}) custom-call(s32[8]{0:T(128)S(1)} %concatenate.11.refs_0_, bf16[1024,256]{1,0:T(8,128)(2,1)S(1)} %fusion.7.refs_1_, bf16[1024,512]{1,0:T(8,128)(2,1)S(1)} %fusion.4.refs_2_), custom_call_target="tpu_custom_call" | custom-call | flops 1342177280 | bytes 4194304 | tf_op jit(solution)/shard_map/pallas_call | solution.py:101
  124.9 10.3 %collective-permute-done.refs_2_ = bf16[1024,512]{1,0:T(8,128)(2,1)S(1)} collective-permute-done((bf16[1024,512]{1,0:T(8,128)(2,1)S(1)}, bf16[1024,512]{1,0:T(8,128)(2,1)S(1)}, u32[]{:S(2)}, u32[]{:S(2)}) %collective-permute-start) | collective-permute-done | bytes 1048608 | tf_op jit(solution)/shard_map/ppermute | solution.py:132
  135.1 0.0 collective-permute-done.1.refs_3_
  135.1 6.0 %shard_map.47 = bf16[1024,256]{1,0:T(8,128)(2,1)} custom-call(s32[10]{0:T(128)S(1)} %pad_add_fusion.1.refs_0_, bf16[1024,256]{1,0:T(8,128)(2,1)S(1)} %fusion.7.refs_1_, bf16[1024,512]{1,0:T(8,128)(2,1)S(1)} %collective-permute-done.refs_2_, bf16[1024,512]{1,0:T(8,128)(2,1)S(1)} %collective-permute-done.1.refs_3_, f32[1024,512]{1,0:T(8,128)S(1)} %get-tuple-element.9.refs_4_, ...), custom_call_target="tpu_custom_call" | custom-call | flops 2684354560 | bytes 5242880 | tf_op jit(solution)/shard_map/pallas_call | solution.py:101
  (1 shorter events, 0.0 us)
Async XLA Ops:
  6.5 94.1 %all-gather.2.cloned.1.call-start = ((), (), s32[]{:S(2)}) async-start(), calls=%async_computation.1 | async-start | bytes 5013504 | tf_op jit(solution)/shard_map/all_gather | solution.py:124
  18.4 10.6 %copy-start.1 = (s32[64]{0:T(128)S(1)}, s32[64]{0:T(128)}, u32[]{:S(2)}) copy-start(s32[64]{0:T(128)} %param.7) | copy-start | bytes 772
  18.4 82.3 %all-to-all-start = ((bf16[8,128,3072]{2,1,0:T(8,128)(2,1)}), bf16[8,128,3072]{2,1,0:T(8,128)(2,1)}, u32[]{:S(2)}, u32[]{:S(2)}) async-start(bf16[8,128,3072]{2,1,0:T(8,128)(2,1)} %broadcast_in_dim.8), calls=%async_computation | async-start | bytes 12582912 | tf_op jit(solution)/shard_map/all_to_all | solution.py:128
  100.7 15.8 %copy-start = (s32[2,3]{1,0:T(2,128)S(1)}, s32[2,3]{1,0:T(2,128)}, u32[]{:S(2)}) copy-start(s32[2,3]{1,0:T(2,128)} %param.6) | copy-start | bytes 76
  107.8 27.4 %collective-permute-start = (bf16[1024,512]{1,0:T(8,128)(2,1)S(1)}, bf16[1024,512]{1,0:T(8,128)(2,1)S(1)}, u32[]{:S(2)}, u32[]{:S(2)}) collective-permute-start(bf16[1024,512]{1,0:T(8,128)(2,1)S(1)} %fusion.4.refs_2_), channel_id=1, source_target_pairs={{0,8},{8,16},{16,24},{24,32},{32,40},{40,48},{48,56},{56,64},{64,7... | collective-permute-start | bytes 3145736 | tf_op jit(solution)/shard_map/ppermute | solution.py:132
  109.7 25.4 %collective-permute-start.1 = (bf16[1024,512]{1,0:T(8,128)(2,1)S(1)}, bf16[1024,512]{1,0:T(8,128)(2,1)S(1)}, u32[]{:S(2)}, u32[]{:S(2)}) collective-permute-start(bf16[1024,512]{1,0:T(8,128)(2,1)S(1)} %fusion.4.refs_2_), channel_id=1, source_target_pairs={{8,0},{16,8},{24,16},{32,24},{40,32},{48,40},{56,48},{64,56},{72,6... | collective-permute-start | bytes 3145736 | tf_op jit(solution)/shard_map/ppermute | solution.py:133
Sparse Core Ops, SparseCore 0:
  13.9 84.4 all-gather.1

commit v2 on v1

v2 whole, which is shorter than its diff:
```python
import functools
import math

import jax
import jax.numpy as jnp
from jax import lax
from jax.experimental import pallas as pl
from jax.experimental.pallas import tpu as pltpu
from jax.sharding import PartitionSpec as P

HD = 128
TH = 8
TW = 8
COLS = 32
TILE = TH * COLS
NEG = -1e30
SCALE = math.log2(math.e) / math.sqrt(HD)
GROUP = 4


def key_marks(tile, reach_row, reach_col, bias):
    lane = lax.broadcasted_iota(jnp.int32, (TILE, HD), 1)
    col = (lax.broadcasted_iota(jnp.int32, (TILE, HD), 0) % COLS) // TW
    by_col = jnp.where(jnp.abs(lane - col) <= reach_col, 0.0, NEG)
    by_row = jnp.where(jnp.abs(lane - 4 - tile) <= reach_row, 0.0, NEG)
    marks = jnp.where(lane < 4, by_col, jnp.where(lane < 8, by_row, jnp.where(lane == 8, bias, 0.0)))
    return marks.astype(jnp.bfloat16)


def query_marks(tile):
    lane = lax.broadcasted_iota(jnp.int32, (TILE, HD), 1)
    col = (lax.broadcasted_iota(jnp.int32, (TILE, HD), 0) % COLS) // TW
    hot = (lane == col) | (lane == 4 + tile) | (lane == 8)
    return hot.astype(jnp.float32).astype(jnp.bfloat16)


def attend_kernel(heads, frames, first, final, tiles, *refs):
    flags, q = refs[0], refs[1]
    kvs = refs[2 : 2 + frames * len(heads)]
    rest = refs[2 + frames * len(heads) :]
    if not first:
        acc_in, top_in = rest[0], rest[1]
        rest = rest[2:]
    if final and len(heads) == 1:
        done, rest = rest[0], rest[1:]
    own = flags[6 + 2 * frames]
    half = TILE // 2

    def put(t, low, value):
        for part, at in ((0, own), (1, 1 - own)):
            place = pl.multiple_of(t * TILE + at * half, half)
            rest[0][pl.ds(place, half), low : low + HD] = value[part * half : (part + 1) * half]

    ones = jnp.ones((TILE, HD), jnp.bfloat16)
    marks = [query_marks(t) for t in range(tiles)]
    for slot, h in enumerate(heads):
        keys, values = [], []
        for i in range(frames):
            bias = jnp.where(flags[6 + 2 * i + h] != 0, 0.0, NEG)
            kv = kvs[i * len(heads) + slot]
            for t in range(tiles):
                rows = pl.ds(t * TILE, TILE)
                mark = key_marks(t, flags[h * 3 + 1], flags[h * 3 + 2], bias)
                keys.append(jnp.concatenate([kv[rows, :HD], mark], axis=1))
                values.append(jnp.concatenate([kv[rows, HD:], ones], axis=1))
        for t in range(tiles):
            rows = pl.ds(t * TILE, TILE)
            query = jnp.concatenate([q[rows, h * HD : (h + 1) * HD], marks[t]], axis=1)
            near = [i * tiles + u for i in range(frames) for u in range(max(t - 1, 0), min(t + 2, tiles))]
            scores = [
                lax.dot_general(
                    query, keys[j], (((1,), (1,)), ((), ())), preferred_element_type=jnp.float32
                )
                for j in near
            ]
            top = functools.reduce(jnp.maximum, scores)
            top = jnp.max(top, axis=1, keepdims=True)
            if not first:
                old = top_in[rows, h : h + 1]
                top = jnp.maximum(top, old)
            shift = top * SCALE
            weight = jnp.concatenate(
                [jnp.exp2(s * SCALE - shift).astype(jnp.bfloat16) for s in scores], axis=1
            )
            value = jnp.concatenate([values[j] for j in near], axis=0)
            acc = jnp.dot(weight, value, preferred_element_type=jnp.float32)
            wide = slice(2 * h * HD, 2 * (h + 1) * HD)
            if not first:
                acc = acc + acc_in[rows, wide] * jnp.exp2(old * SCALE - shift)
            if not final:
                rest[0][rows, wide] = acc
                rest[1][rows, h : h + 1] = top
            elif len(heads) == 1 and h == 0:
                rest[0][rows, :] = (acc[:, :HD] / acc[:, HD:]).astype(jnp.bfloat16)
            else:
                put(t, h * HD, (acc[:, :HD] / acc[:, HD:]).astype(jnp.bfloat16))
                if len(heads) == 1:
                    put(t, 0, done[rows, :])


def attend(heads, flags, q, kvs, state=None, final=True, done=None):
    tokens = q.shape[0]
    frames = len(kvs)
    vmem = pl.BlockSpec(memory_space=pltpu.VMEM)
    arrays = [q, *(part for kv in kvs for part in kv), *(state or ())]
    if done is not None:
        arrays.append(done)
    elif final:
        arrays.append(jnp.zeros((16, HD), jnp.bfloat16))
    if final:
        out = jax.ShapeDtypeStruct((tokens, HD if done is None else 2 * HD), jnp.bfloat16)
    else:
        out = (
            jax.ShapeDtypeStruct((tokens, 4 * HD), jnp.float32),
            jax.ShapeDtypeStruct((tokens, HD), jnp.float32),
        )
    pairs = frames * len(heads) * 10 * TILE * TILE
    return pl.pallas_call(
        functools.partial(attend_kernel, heads, frames, state is None, final, tokens // TILE),
        out_shape=out,
        in_specs=[pl.BlockSpec(memory_space=pltpu.SMEM)] + [vmem] * len(arrays),
        out_specs=vmem if final else (vmem, vmem),
        compiler_params=pltpu.CompilerParams(vmem_limit_bytes=40 * 1024 * 1024),
        cost_estimate=pl.CostEstimate(
            flops=pairs * 1024, bytes_accessed=(frames + 3) << 19, transcendentals=pairs
        ),
    )(flags, *arrays)


def order_kernel(turns, where, *refs):
    out, done = refs[-2:]
    step = TILE // 2
    copies = []
    for i, block in enumerate(refs[:-2]):
        y = lax.rem(where[2] + turns[i // 2], len(turns))
        to = pl.ds(pl.multiple_of(y * TILE + i % 2 * step, step), step)
        copy = pltpu.make_async_copy(block, out.at[to, :], done.at[i])
        copy.start()
        copies.append(copy)
    for copy in copies:
        copy.wait()


def order(where, near, far, turns):
    blocks = [block for pair in zip(near, far) for block in pair]
    step, features = blocks[0].shape
    return pl.pallas_call(
        functools.partial(order_kernel, turns),
        out_shape=jax.ShapeDtypeStruct((len(blocks) * step, features), jnp.bfloat16),
        in_specs=[pl.BlockSpec(memory_space=pltpu.SMEM)]
        + [pl.BlockSpec(memory_space=pl.ANY)] * len(blocks),
        out_specs=pl.BlockSpec(memory_space=pltpu.VMEM),
        scratch_shapes=[pltpu.SemaphoreType.DMA((len(blocks),))],
        compiler_params=pltpu.CompilerParams(vmem_limit_bytes=16 * 1024 * 1024),
        cost_estimate=pl.CostEstimate(flops=1 << 20, bytes_accessed=12 << 20, transcendentals=0),
    )(where, *blocks)


def project_kernel(*refs):
    parts, tokens, out = refs[:-2], refs[-2], refs[-1]
    if len(parts) == 1:
        matrix = parts[0][...]
    else:
        depth = parts[0].shape[0] // 2
        heads = [
            jnp.concatenate([part[h * depth : (h + 1) * depth, :] for part in parts], axis=0)
            for h in range(2)
        ]
        matrix = jnp.concatenate(heads, axis=1)
    step = 512
    for i in range(0, tokens.shape[0], step):
        rows = pl.ds(i, step)
        result = jnp.dot(tokens[rows, :], matrix, preferred_element_type=jnp.float32)
        out[rows, :] = result.astype(jnp.bfloat16)


def project(parts, tokens):
    rows, features = tokens.shape
    columns = 2 * HD
    vmem = pl.BlockSpec(memory_space=pltpu.VMEM)
    return pl.pallas_call(
        project_kernel,
        out_shape=jax.ShapeDtypeStruct((rows, columns), jnp.bfloat16),
        in_specs=[vmem] * (len(parts) + 1),
        out_specs=vmem,
        compiler_params=pltpu.CompilerParams(vmem_limit_bytes=20 * 1024 * 1024),
        cost_estimate=pl.CostEstimate(
            flops=2 * rows * features * columns,
            bytes_accessed=2 * (rows * features + features * columns),
            transcendentals=0,
        ),
    )(*parts, tokens)


def body(frames, row_count, video, qkv_weight, window, clips):
    axes = ("frame", "row")
    frame_here = lax.axis_index("frame").astype(jnp.int32)
    row_here = lax.axis_index("row").astype(jnp.int32)
    depth = frames // GROUP
    y_count = row_count // 2
    width = qkv_weight.shape[2]
    share = qkv_weight.shape[0]
    features = video.shape[3]

    def send(value, to):
        pairs = []
        for f in range(frames):
            for r in range(row_count):
                tf, tr = to(f, r)
                pairs.append((f * row_count + r, tf * row_count + tr))
        return lax.ppermute(value, axes, pairs)

    other_x_hi = lambda value: send(value, lambda f, r: (f, r ^ 1))

    columns = [[g * GROUP + i for g in range(depth)] for i in range(GROUP)]
    four = [[g * GROUP + i for i in range(GROUP)] for g in range(depth)]

    shard = qkv_weight.reshape(share, 3 * width)
    cut = lambda j, h: shard[:, j * width + h * HD : j * width + (h + 1) * HD]
    shard = jnp.concatenate([cut(1, 0), cut(2, 0), cut(1, 1), cut(2, 1), shard[:, :width]], axis=1)
    group = lax.all_gather(shard, "frame", axis=0, tiled=True, axis_index_groups=four)
    mine = lax.dynamic_slice_in_dim(group, 4 * HD + frame_here % 2 * HD, HD, 1)
    group = jnp.concatenate([group[:, : 4 * HD], mine], axis=1)
    matrix = lax.all_gather(group, "frame", axis=0, tiled=True, axis_index_groups=columns)

    block = video.reshape(-1, features)
    block, group = lax.optimization_barrier((block, group))
    along_y = lambda value, k: send(value, lambda f, r: (f, (r - 2 * k) % row_count))
    turns = (0, 1, y_count - 1, 2)
    block_x = other_x_hi(block)
    near = [block] + [along_y(block, k) for k in turns[1:]]
    far = [block_x, along_y(block_x, 1), along_y(block_x, -1), other_x_hi(near[3])]

    where = jnp.stack([frame_here // 2 % 2, frame_here % 2, row_here // 2])
    tokens = order(where, near, far, turns)
    up = [(i, i + 1) for i in range(frames - 1)]
    down = [(j, i) for i, j in up]
    kv, before, after = [], [], []
    for h in range(2):
        result = project([matrix[:, h * 2 * HD : (h + 1) * 2 * HD]], tokens)
        kv.append(result)
        before.append(lax.ppermute(result, "frame", up))
        after.append(lax.ppermute(result, "frame", down))
    mine, *_ = lax.optimization_barrier((matrix[:, 4 * HD :], *kv))
    pairs = [[f, f + 1] for f in range(0, frames, 2)]
    halves = [
        lax.all_gather(half, "frame", axis=0, tiled=True, axis_index_groups=pairs)
        for half in jnp.split(mine, 2, axis=0)
    ]
    q = project(halves, tokens)

    edge = jnp.full((1,), -1, jnp.int32)
    near_clips = lax.dynamic_slice_in_dim(jnp.concatenate([edge, clips, edge]), frame_here, 3, 0)
    reach = window[:, 0]
    flag = lambda side: ((reach >= 1) & (near_clips[side] == near_clips[1])).astype(jnp.int32)
    head = window.reshape(-1)
    place = (row_here % 2).reshape(1)
    here = jnp.concatenate([head, jnp.ones((2,), jnp.int32), place])
    sides = jnp.concatenate([head, flag(0), flag(2), place])

    state = attend((0, 1), here, q, [kv], None, False)
    done = attend((0,), sides, q, [before[:1], after[:1]], state)
    out = attend((1,), sides, q, [before[1:], after[1:]], state, True, done)
    return out.reshape(1, row_count * video.shape[1], -1, width)


def solution(mesh):
    placed = (P("frame", "row", None, None), P("frame", None, "row"), P("row", None), P())
    sizes = (mesh.shape["frame"], mesh.shape["row"])
    return jax.shard_map(
        functools.partial(body, *sizes), mesh=mesh,
        in_specs=placed,
        out_specs=P("frame", None, None, "row"),
        check_vma=False,
    )
```

time: 150 us -> 141 us (0.940); the launches traced: 148 us -> 141 us
  waiting for transfers between devices: 81.8 us -> 47.8 us
  starting transfers between devices: 16.2 us -> 36.6 us
  matrix products: 12.1 us -> 0 us
  Pallas kernels: 9.07 us -> 17.6 us
  blocking collectives: 6.31 us -> 10.8 us
  local copies, waits for them, and re-layouts: 6.28 us -> 9.02 us
  other arithmetic: 0.3 us -> 2.51 us
    all_to_all x1 -> x0, waiting for transfers between devices: 71.5 us -> none  [body(): tokens = lax.all_to_all(copies, 'row', 0, 0).reshape(-1, features)]
    ppermute x2 -> x11, starting transfers between devices: 5.56 us -> 36.6 us  [the longest x7 26.5 us: send(): return lax.ppermute(value, axes, pairs)]
    ppermute x2 -> x11, waiting for transfers between devices: 10.3 us -> 35.5 us  [the longest x7 32.2 us: send(): return lax.ppermute(value, axes, pairs)]
    all_gather x1, waiting for transfers between devices: 0.01 us -> 12.4 us  [body(): lax.all_gather(group, 'frame', axis=0, tiled=True, axis_index_groups=colu...]
    dot_general x2 -> x0, matrix products: 12.1 us -> none  [the longest x1 7.12 us: body(): jnp.dot(tokens, matrix[:, width:], preferred_element_type=jnp.float32)]
    all_to_all x1 -> x0, starting transfers between devices: 10.6 us -> none  [body(): tokens = lax.all_to_all(copies, 'row', 0, 0).reshape(-1, features)]
    pallas_call x2 -> x7, Pallas kernels: 9.07 us -> 17.6 us  [the longest x3 9.58 us: attend(): pl.pallas_call(functools.partial(attend_kernel, heads, frames, state is N...]
    broadcast_in_dim x1, local copies, waits for them, and re-layouts: 4.62 us -> 0.01 us  [attend(): arrays.append(jnp.zeros((16, HD), jnp.bfloat16))]
  transfers between devices with their start and end apart: 4 -> 12, of which waited for: 2 -> 8; matrix products, arithmetic and copies ran while one was open for 7% -> 2% of each run, Pallas kernels for 2% -> 9%
where the time goes in v2:
time: 141 us
  waiting for transfers between devices  47.8 us (34%)
  starting transfers between devices  36.6 us (26%)
  Pallas kernels  17.6 us (12%)
  between operations  16.3 us (12%)
  blocking collectives  10.8 us (8%)
  local copies, waits for them, and re-layouts  9.02 us (6%)
  other arithmetic  2.51 us (2%)
    ppermute x7, waiting for transfers between devices, send(): return lax.ppermute(value, axes, pairs)  32.2 us
    ppermute x7, starting transfers between devices, send(): return lax.ppermute(value, axes, pairs)  26.5 us
    all_gather x1, waiting for transfers between devices, body(): lax.all_gather(group, 'frame', axis=0, tiled=True, axis_index_groups=colu...  12.4 us
    pallas_call x3, Pallas kernels, attend(): pl.pallas_call(functools.partial(attend_kernel, heads, frames, state is N...  9.58 us
    ppermute x2, starting transfers between devices, body(): before.append(lax.ppermute(result, 'frame', up))  5.98 us
    all_gather x1, blocking collectives, body(): lax.all_gather(shard, 'frame', axis=0, tiled=True, axis_index_groups=four)  5.88 us
    pallas_call x3, Pallas kernels, project(): pl.pallas_call(project_kernel, out_shape=jax.ShapeDtypeStruct((rows, colu...  5.35 us
    all_gather x2, blocking collectives, body(): lax.all_gather(half, 'frame', axis=0, tiled=True, axis_index_groups=pairs)  4.91 us
  transfers between devices with their start and end apart: 12, of which 8 were waited for; matrix products, arithmetic and copies ran while one was open for 2% of the time, Pallas kernels for 9%

profile of v2, /device:TPU:6, one launch (start us, length us, event | category | flops | bytes accessed | tf_op | source)
XLA Modules:
  0.0 140.6 jit_solution(14300321193484262758)
XLA Ops:
  6.5 1.0 copy.7
  7.6 5.9 %all_gather.12 = bf16[192,768]{1,0:T(8,128)(2,1)S(1)} all-gather(bf16[48,768]{1,0:T(8,128)(2,1)S(1)} %slice_dynamic-update-slice_fusion), channel_id=1, replica_groups={{0,8,16,24},{32,40,48,56},{64,72,80,88},{96,104,112,120},{128,136,144,1..., dimensions={0}, use_global_device_ids=true | all-gather | bytes 368640 | tf_op jit(solution)/shard_map/all_gather | solution.py:221
  14.2 7.8 %collective-permute-start = (bf16[128,3072]{1,0:T(8,128)(2,1)}, bf16[128,3072]{1,0:T(8,128)(2,1)S(1)}, u32[]{:S(2)}, u32[]{:S(2)}) collective-permute-start(bf16[128,3072]{1,0:T(8,128)(2,1)} %bitcast.10), channel_id=1, source_target_pairs={{0,1},{1,0},{2,3},{3,2},{4,5},{5,4},{6,7},{7,6},{8,9},{9,8},{10,11... | collective-permute-start | bytes 2359304 | tf_op jit(solution)/shard_map/ppermute | solution.py:211
  22.0 1.9 %collective-permute-start.5 = (bf16[128,3072]{1,0:T(8,128)(2,1)}, bf16[128,3072]{1,0:T(8,128)(2,1)S(1)}, u32[]{:S(2)}, u32[]{:S(2)}) collective-permute-start(bf16[128,3072]{1,0:T(8,128)(2,1)} %bitcast.11), channel_id=1, source_target_pairs={{0,4},{1,5},{2,6},{3,7},{4,0},{5,1},{6,2},{7,3},{8,12},{9,13},{10,... | collective-permute-start | bytes 2359304 | tf_op jit(solution)/shard_map/ppermute | solution.py:211
  23.9 1.9 %collective-permute-start.1 = (bf16[128,3072]{1,0:T(8,128)(2,1)}, bf16[128,3072]{1,0:T(8,128)(2,1)S(1)}, u32[]{:S(2)}, u32[]{:S(2)}) collective-permute-start(bf16[128,3072]{1,0:T(8,128)(2,1)} %bitcast.12), channel_id=1, source_target_pairs={{0,6},{1,7},{2,0},{3,1},{4,2},{5,3},{6,4},{7,5},{8,14},{9,15},{10,... | collective-permute-start | bytes 2359304 | tf_op jit(solution)/shard_map/ppermute | solution.py:211
  25.9 3.9 %collective-permute-start.3 = (bf16[128,3072]{1,0:T(8,128)(2,1)}, bf16[128,3072]{1,0:T(8,128)(2,1)}, u32[]{:S(2)}, u32[]{:S(2)}) collective-permute-start(bf16[128,3072]{1,0:T(8,128)(2,1)} %bitcast.13), channel_id=1, source_target_pairs={{0,2},{1,3},{2,4},{3,5},{4,6},{5,7},{6,0},{7,1},{8,10},{9,11},{10,... | collective-permute-start | bytes 2359304 | tf_op jit(solution)/shard_map/ppermute | solution.py:211
  29.8 10.5 %collective-permute-done.refs_1_ = bf16[128,3072]{1,0:T(8,128)(2,1)S(1)} collective-permute-done((bf16[128,3072]{1,0:T(8,128)(2,1)}, bf16[128,3072]{1,0:T(8,128)(2,1)S(1)}, u32[]{:S(2)}, u32[]{:S(2)}) %collective-permute-start) | collective-permute-done | bytes 786464 | tf_op jit(solution)/shard_map/ppermute | solution.py:211
  40.3 2.3 %collective-permute-start.2 = (bf16[128,3072]{1,0:T(8,128)(2,1)S(1)}, bf16[128,3072]{1,0:T(8,128)(2,1)}, u32[]{:S(2)}, u32[]{:S(2)}) collective-permute-start(bf16[128,3072]{1,0:T(8,128)(2,1)S(1)} %collective-permute-done.refs_1_), channel_id=1, source_target_pairs={{0,6},{1,7},{2,0},{3,1},{4,2},{5,3},{6,4},{7,5},{8,14},{9,15},{10,... | collective-permute-start | bytes 2359304 | tf_op jit(solution)/shard_map/ppermute | solution.py:211
  42.5 3.6 %collective-permute-start.4 = (bf16[128,3072]{1,0:T(8,128)(2,1)S(1)}, bf16[128,3072]{1,0:T(8,128)(2,1)}, u32[]{:S(2)}, u32[]{:S(2)}) collective-permute-start(bf16[128,3072]{1,0:T(8,128)(2,1)S(1)} %collective-permute-done.refs_1_), channel_id=1, source_target_pairs={{0,2},{1,3},{2,4},{3,5},{4,6},{5,7},{6,0},{7,1},{8,10},{9,11},{10,... | collective-permute-start | bytes 2359304 | tf_op jit(solution)/shard_map/ppermute | solution.py:211
  46.1 5.1 %collective-permute-start.6 = (bf16[128,3072]{1,0:T(8,128)(2,1)S(1)}, bf16[128,3072]{1,0:T(8,128)(2,1)}, u32[]{:S(2)}, u32[]{:S(2)}) collective-permute-start(bf16[128,3072]{1,0:T(8,128)(2,1)S(1)} %collective-permute-done.5.refs_6_), channel_id=1, source_target_pairs={{0,1},{1,0},{2,3},{3,2},{4,5},{5,4},{6,7},{7,6},{8,9},{9,8},{10,11... | collective-permute-start | bytes 2359304 | tf_op jit(solution)/shard_map/ppermute | solution.py:211
  57.2 1.6 %collective-permute-done.1.refs_2_ = bf16[128,3072]{1,0:T(8,128)(2,1)S(1)} collective-permute-done((bf16[128,3072]{1,0:T(8,128)(2,1)}, bf16[128,3072]{1,0:T(8,128)(2,1)S(1)}, u32[]{:S(2)}, u32[]{:S(2)}) %collective-permute-start.1) | collective-permute-done | bytes 786464 | tf_op jit(solution)/shard_map/ppermute | solution.py:211
  58.8 3.4 %collective-permute-done.3.refs_4_ = bf16[128,3072]{1,0:T(8,128)(2,1)} collective-permute-done((bf16[128,3072]{1,0:T(8,128)(2,1)}, bf16[128,3072]{1,0:T(8,128)(2,1)}, u32[]{:S(2)}, u32[]{:S(2)}) %collective-permute-start.3) | collective-permute-done | bytes 786464 | tf_op jit(solution)/shard_map/ppermute | solution.py:211
  62.2 12.7 %collective-permute-done.2.refs_3_ = bf16[128,3072]{1,0:T(8,128)(2,1)} collective-permute-done((bf16[128,3072]{1,0:T(8,128)(2,1)S(1)}, bf16[128,3072]{1,0:T(8,128)(2,1)}, u32[]{:S(2)}, u32[]{:S(2)}) %collective-permute-start.2) | collective-permute-done | bytes 786464 | tf_op jit(solution)/shard_map/ppermute | solution.py:211
  74.9 4.1 %collective-permute-done.4.refs_5_ = bf16[128,3072]{1,0:T(8,128)(2,1)} collective-permute-done((bf16[128,3072]{1,0:T(8,128)(2,1)S(1)}, bf16[128,3072]{1,0:T(8,128)(2,1)}, u32[]{:S(2)}, u32[]{:S(2)}) %collective-permute-start.4) | collective-permute-done | bytes 786464 | tf_op jit(solution)/shard_map/ppermute | solution.py:211
  78.9 2.7 %shard_map.46.refs_1_.refs_2_ = bf16[1024,3072]{1,0:T(8,128)(2,1)S(1)} custom-call(s32[3]{0:T(128)S(1)} %pad_add_fusion.2.where, bf16[128,3072]{1,0:T(8,128)(2,1)S(1)} %bitcast.14, bf16[128,3072]{1,0:T(8,128)(2,1)S(1)} %collective-permute-done.refs_1_, bf16[128,3072]{1,0:T(8,128)(2,1)S(1)} %collective-permute-done.1.refs_2_, ...), custom_call_target="tpu_custom_call" | custom-call | flops 1048576 | bytes 12582912 | tf_op jit(solution)/shard_map/pallas_call | solution.py:147
  81.7 2.6 %copy-done = bf16[1024,3072]{1,0:T(8,128)(2,1)} copy-done((bf16[1024,3072]{1,0:T(8,128)(2,1)}, bf16[1024,3072]{1,0:T(8,128)(2,1)S(1)}, u32[]{:S(2)}) %copy-start) | copy-done | bytes 6291480
  84.3 12.4 %all-gather.2.cloned.1.call-done = bf16[3072,640]{1,0:T(8,128)(2,1)} async-done(((bf16[192,640]{1,0:T(8,128)(2,1)}), bf16[3072,640]{1,0:T(8,128)(2,1)}) %all-gather.2.cloned.1.call-update) | async-done | bytes 3932176 | tf_op jit(solution)/shard_map/all_gather | solution.py:224
  96.7 2.3 %fusion.2 = (bf16[3072,256]{1,0:T(8,128)(2,1)S(1)}, bf16[3072,256]{1,0:T(8,128)(2,1)S(1)}) fusion(bf16[3072,640]{1,0:T(8,128)(2,1)} %all-gather.2.cloned.1.call-done), kind=kLoop, calls=%fused_computation.16 | loop fusion | bytes 6291456 | tf_op jit(solution)/shard_map/slice | solution.py:240
  98.9 1.5 %copy-done.1 = bf16[1024,3072]{1,0:T(8,128)(2,1)S(1)} copy-done((bf16[1024,3072]{1,0:T(8,128)(2,1)S(1)}, bf16[1024,3072]{1,0:T(8,128)(2,1)}, u32[]{:S(2)}) %copy-start.1) | copy-done | bytes 6291480
  100.4 1.8 %shard_map.47.refs_2_ = bf16[1024,256]{1,0:T(8,128)(2,1)S(1)} custom-call(bf16[3072,256]{1,0:T(8,128)(2,1)S(1)} %get-tuple-element.16.refs_0_, bf16[1024,3072]{1,0:T(8,128)(2,1)S(1)} %copy-done.1), custom_call_target="tpu_custom_call" | custom-call | flops 1610612736 | bytes 7864320 | tf_op jit(solution)/shard_map/pallas_call | solution.py:181
  102.2 1.9 %collective-permute-start.10 = (bf16[1024,256]{1,0:T(8,128)(2,1)S(1)}, bf16[1024,256]{1,0:T(8,128)(2,1)S(1)}, u32[]{:S(2)}, u32[]{:S(2)}) collective-permute-start(bf16[1024,256]{1,0:T(8,128)(2,1)S(1)} %shard_map.47.refs_2_), channel_id=1, source_target_pairs={{8,0},{16,8},{24,16},{32,24},{40,32},{48,40},{56,48},{64,56},{72,6... | collective-permute-start | bytes 1572872 | tf_op jit(solution)/shard_map/ppermute | solution.py:243
  104.2 2.4 %collective-permute-start.9 = (bf16[1024,256]{1,0:T(8,128)(2,1)S(1)}, bf16[1024,256]{1,0:T(8,128)(2,1)S(1)}, u32[]{:S(2)}, u32[]{:S(2)}) collective-permute-start(bf16[1024,256]{1,0:T(8,128)(2,1)S(1)} %shard_map.47.refs_2_), channel_id=1, source_target_pairs={{0,8},{8,16},{16,24},{24,32},{32,40},{40,48},{48,56},{56,64},{64,7... | collective-permute-start | bytes 1572872 | tf_op jit(solution)/shard_map/ppermute | solution.py:242
  106.6 1.8 %shard_map.48.refs_3_ = bf16[1024,256]{1,0:T(8,128)(2,1)S(1)} custom-call(bf16[3072,256]{1,0:T(8,128)(2,1)S(1)} %get-tuple-element.15.refs_0_, bf16[1024,3072]{1,0:T(8,128)(2,1)S(1)} %copy-done.1), custom_call_target="tpu_custom_call" | custom-call | flops 1610612736 | bytes 7864320 | tf_op jit(solution)/shard_map/pallas_call | solution.py:181
  108.4 3.6 %collective-permute-start.7 = (bf16[1024,256]{1,0:T(8,128)(2,1)S(1)}, bf16[1024,256]{1,0:T(8,128)(2,1)S(1)}, u32[]{:S(2)}, u32[]{:S(2)}) collective-permute-start(bf16[1024,256]{1,0:T(8,128)(2,1)S(1)} %shard_map.48.refs_3_), channel_id=1, source_target_pairs={{0,8},{8,16},{16,24},{24,32},{32,40},{40,48},{48,56},{56,64},{64,7... | collective-permute-start | bytes 1572872 | tf_op jit(solution)/shard_map/ppermute | solution.py:242
  112.0 2.1 %collective-permute-start.8 = (bf16[1024,256]{1,0:T(8,128)(2,1)S(1)}, bf16[1024,256]{1,0:T(8,128)(2,1)S(1)}, u32[]{:S(2)}, u32[]{:S(2)}) collective-permute-start(bf16[1024,256]{1,0:T(8,128)(2,1)S(1)} %shard_map.48.refs_3_), channel_id=1, source_target_pairs={{8,0},{16,8},{24,16},{32,24},{40,32},{48,40},{56,48},{64,56},{72,6... | collective-permute-start | bytes 1572872 | tf_op jit(solution)/shard_map/ppermute | solution.py:243
  114.1 2.4 %all_gather.14.refs_0_ = bf16[3072,128]{1,0:T(8,128)(2,1)S(1)} all-gather(bf16[1536,128]{1,0:T(8,128)(2,1)S(1)} %get-tuple-element.18), channel_id=1, replica_groups={{0,8},{16,24},{32,40},{48,56},{64,72},{80,88},{96,104},{112,120},{128,1..., dimensions={0}, use_global_device_ids=true | all-gather | bytes 1179648 | tf_op jit(solution)/shard_map/all_gather | solution.py:247
  116.5 2.5 %all_gather.15.refs_1_ = bf16[3072,128]{1,0:T(8,128)(2,1)S(1)} all-gather(bf16[1536,128]{1,0:T(8,128)(2,1)S(1)} %get-tuple-element.17), channel_id=1, replica_groups={{0,8},{16,24},{32,40},{48,56},{64,72},{80,88},{96,104},{112,120},{128,1..., dimensions={0}, use_global_device_ids=true | all-gather | bytes 1179648 | tf_op jit(solution)/shard_map/all_gather | solution.py:247
  119.1 1.8 %shard_map.49.refs_1_ = bf16[1024,256]{1,0:T(8,128)(2,1)S(1)} custom-call(bf16[3072,128]{1,0:T(8,128)(2,1)S(1)} %all_gather.14.refs_0_, bf16[3072,128]{1,0:T(8,128)(2,1)S(1)} %all_gather.15.refs_1_, bf16[1024,3072]{1,0:T(8,128)(2,1)S(1)} %copy-done.1), custom_call_target="tpu_custom_call" | custom-call | flops 1610612736 | bytes 7864320 | tf_op jit(solution)/shard_map/pallas_call | solution.py:181
  120.9 3.1 %shard_map.50 = (f32[1024,512]{1,0:T(8,128)S(1)}, f32[1024,128]{1,0:T(8,128)S(1)}) custom-call(s32[9]{0:T(128)S(1)} %pad_add_fusion.3.refs_0_, bf16[1024,256]{1,0:T(8,128)(2,1)S(1)} %shard_map.49.refs_1_, bf16[1024,256]{1,0:T(8,128)(2,1)S(1)} %shard_map.47.refs_2_, bf16[1024,256]{1,0:T(8,128)(2,1)S(1)} %shard_map.48.refs_3_), custom_call_target="tpu_custom_call" | custom-call | flops 1342177280 | bytes 2097152 | tf_op jit(solution)/shard_map/pallas_call | solution.py:118
  124.4 2.8 %shard_map.51.refs_6_ = bf16[1024,128]{1,0:T(8,128)(2,1)S(1)} custom-call(s32[11]{0:T(128)S(1)} %pad_add_fusion.1.refs_0_, bf16[1024,256]{1,0:T(8,128)(2,1)S(1)} %shard_map.49.refs_1_, bf16[1024,256]{1,0:T(8,128)(2,1)S(1)} %collective-permute-done.9.refs_2_, bf16[1024,256]{1,0:T(8,128)(2,1)S(1)} %collective-permute-done.10.refs_3_, ...), custom_call_target="tpu_custom_call" | custom-call | flops 1342177280 | bytes 2621440 | tf_op jit(solution)/shard_map/pallas_call | solution.py:118
  127.3 2.8 %collective-permute-done.7.refs_2_ = bf16[1024,256]{1,0:T(8,128)(2,1)S(1)} collective-permute-done((bf16[1024,256]{1,0:T(8,128)(2,1)S(1)}, bf16[1024,256]{1,0:T(8,128)(2,1)S(1)}, u32[]{:S(2)}, u32[]{:S(2)}) %collective-permute-start.7) | collective-permute-done | bytes 524320 | tf_op jit(solution)/shard_map/ppermute | solution.py:242
  130.1 3.7 %shard_map.52 = bf16[1024,256]{1,0:T(8,128)(2,1)} custom-call(s32[11]{0:T(128)S(1)} %pad_add_fusion.1.refs_0_, bf16[1024,256]{1,0:T(8,128)(2,1)S(1)} %shard_map.49.refs_1_, bf16[1024,256]{1,0:T(8,128)(2,1)S(1)} %collective-permute-done.7.refs_2_, bf16[1024,256]{1,0:T(8,128)(2,1)S(1)} %collective-permute-done.8.refs_3_, ...), custom_call_target="tpu_custom_call" | custom-call | flops 1342177280 | bytes 2621440 | tf_op jit(solution)/shard_map/pallas_call | solution.py:118
  (32 shorter events, 4.7 us)
Async XLA Ops:
  6.5 72.4 %copy-start.2 = (bf16[1,4,32,3072]{3,2,1,0:T(8,128)(2,1)S(1)}, bf16[1,4,32,3072]{3,2,1,0:T(8,128)(2,1)}, u32[]{:S(2)}) copy-start(bf16[1,4,32,3072]{3,2,1,0:T(8,128)(2,1)} %param.4) | copy-start | bytes 2359300
  6.5 90.1 %all-gather.2.cloned.1.call-start = ((), (), s32[]{:S(2)}) async-start(), calls=%async_computation | async-start | bytes 4177920 | tf_op jit(solution)/shard_map/all_gather | solution.py:224
  14.2 26.0 %collective-permute-start = (bf16[128,3072]{1,0:T(8,128)(2,1)}, bf16[128,3072]{1,0:T(8,128)(2,1)S(1)}, u32[]{:S(2)}, u32[]{:S(2)}) collective-permute-start(bf16[128,3072]{1,0:T(8,128)(2,1)} %bitcast.10), channel_id=1, source_target_pairs={{0,1},{1,0},{2,3},{3,2},{4,5},{5,4},{6,7},{7,6},{8,9},{9,8},{10,11... | collective-permute-start | bytes 2359304 | tf_op jit(solution)/shard_map/ppermute | solution.py:211
  22.0 24.1 %collective-permute-start.5 = (bf16[128,3072]{1,0:T(8,128)(2,1)}, bf16[128,3072]{1,0:T(8,128)(2,1)S(1)}, u32[]{:S(2)}, u32[]{:S(2)}) collective-permute-start(bf16[128,3072]{1,0:T(8,128)(2,1)} %bitcast.11), channel_id=1, source_target_pairs={{0,4},{1,5},{2,6},{3,7},{4,0},{5,1},{6,2},{7,3},{8,12},{9,13},{10,... | collective-permute-start | bytes 2359304 | tf_op jit(solution)/shard_map/ppermute | solution.py:211
  23.9 34.8 %collective-permute-start.1 = (bf16[128,3072]{1,0:T(8,128)(2,1)}, bf16[128,3072]{1,0:T(8,128)(2,1)S(1)}, u32[]{:S(2)}, u32[]{:S(2)}) collective-permute-start(bf16[128,3072]{1,0:T(8,128)(2,1)} %bitcast.12), channel_id=1, source_target_pairs={{0,6},{1,7},{2,0},{3,1},{4,2},{5,3},{6,4},{7,5},{8,14},{9,15},{10,... | collective-permute-start | bytes 2359304 | tf_op jit(solution)/shard_map/ppermute | solution.py:211
  25.9 36.3 %collective-permute-start.3 = (bf16[128,3072]{1,0:T(8,128)(2,1)}, bf16[128,3072]{1,0:T(8,128)(2,1)}, u32[]{:S(2)}, u32[]{:S(2)}) collective-permute-start(bf16[128,3072]{1,0:T(8,128)(2,1)} %bitcast.13), channel_id=1, source_target_pairs={{0,2},{1,3},{2,4},{3,5},{4,6},{5,7},{6,0},{7,1},{8,10},{9,11},{10,... | collective-permute-start | bytes 2359304 | tf_op jit(solution)/shard_map/ppermute | solution.py:211
  40.3 34.6 %collective-permute-start.2 = (bf16[128,3072]{1,0:T(8,128)(2,1)S(1)}, bf16[128,3072]{1,0:T(8,128)(2,1)}, u32[]{:S(2)}, u32[]{:S(2)}) collective-permute-start(bf16[128,3072]{1,0:T(8,128)(2,1)S(1)} %collective-permute-done.refs_1_), channel_id=1, source_target_pairs={{0,6},{1,7},{2,0},{3,1},{4,2},{5,3},{6,4},{7,5},{8,14},{9,15},{10,... | collective-permute-start | bytes 2359304 | tf_op jit(solution)/shard_map/ppermute | solution.py:211
  42.5 36.4 %collective-permute-start.4 = (bf16[128,3072]{1,0:T(8,128)(2,1)S(1)}, bf16[128,3072]{1,0:T(8,128)(2,1)}, u32[]{:S(2)}, u32[]{:S(2)}) collective-permute-start(bf16[128,3072]{1,0:T(8,128)(2,1)S(1)} %collective-permute-done.refs_1_), channel_id=1, source_target_pairs={{0,2},{1,3},{2,4},{3,5},{4,6},{5,7},{6,0},{7,1},{8,10},{9,11},{10,... | collective-permute-start | bytes 2359304 | tf_op jit(solution)/shard_map/ppermute | solution.py:211
  46.1 32.8 %collective-permute-start.6 = (bf16[128,3072]{1,0:T(8,128)(2,1)S(1)}, bf16[128,3072]{1,0:T(8,128)(2,1)}, u32[]{:S(2)}, u32[]{:S(2)}) collective-permute-start(bf16[128,3072]{1,0:T(8,128)(2,1)S(1)} %collective-permute-done.5.refs_6_), channel_id=1, source_target_pairs={{0,1},{1,0},{2,3},{3,2},{4,5},{5,4},{6,7},{7,6},{8,9},{9,8},{10,11... | collective-permute-start | bytes 2359304 | tf_op jit(solution)/shard_map/ppermute | solution.py:211
  81.6 2.7 %copy-start = (bf16[1024,3072]{1,0:T(8,128)(2,1)}, bf16[1024,3072]{1,0:T(8,128)(2,1)S(1)}, u32[]{:S(2)}) copy-start(bf16[1024,3072]{1,0:T(8,128)(2,1)S(1)} %shard_map.46.refs_1_.refs_2_) | copy-start | bytes 18874372
  96.7 3.8 %copy-start.1 = (bf16[1024,3072]{1,0:T(8,128)(2,1)S(1)}, bf16[1024,3072]{1,0:T(8,128)(2,1)}, u32[]{:S(2)}) copy-start(bf16[1024,3072]{1,0:T(8,128)(2,1)} %copy-done) | copy-start | bytes 18874372
  102.2 21.7 %collective-permute-start.10 = (bf16[1024,256]{1,0:T(8,128)(2,1)S(1)}, bf16[1024,256]{1,0:T(8,128)(2,1)S(1)}, u32[]{:S(2)}, u32[]{:S(2)}) collective-permute-start(bf16[1024,256]{1,0:T(8,128)(2,1)S(1)} %shard_map.47.refs_2_), channel_id=1, source_target_pairs={{8,0},{16,8},{24,16},{32,24},{40,32},{48,40},{56,48},{64,56},{72,6... | collective-permute-start | bytes 1572872 | tf_op jit(solution)/shard_map/ppermute | solution.py:243
  104.2 20.3 %collective-permute-start.9 = (bf16[1024,256]{1,0:T(8,128)(2,1)S(1)}, bf16[1024,256]{1,0:T(8,128)(2,1)S(1)}, u32[]{:S(2)}, u32[]{:S(2)}) collective-permute-start(bf16[1024,256]{1,0:T(8,128)(2,1)S(1)} %shard_map.47.refs_2_), channel_id=1, source_target_pairs={{0,8},{8,16},{16,24},{24,32},{32,40},{40,48},{48,56},{56,64},{64,7... | collective-permute-start | bytes 1572872 | tf_op jit(solution)/shard_map/ppermute | solution.py:242
  108.4 5.7 %slice-start = ((bf16[3072,640]{1,0:T(8,128)(2,1)}), bf16[3072,128]{1,0:T(8,128)(2,1)S(1)}, s32[]{:S(2)}) async-start(bf16[3072,640]{1,0:T(8,128)(2,1)} %all-gather.2.cloned.1.call-done), calls=%async_computation.1 | async-start | bytes 1572864 | tf_op jit(solution)/shard_map/slice | solution.py:244
  108.4 21.7 %collective-permute-start.7 = (bf16[1024,256]{1,0:T(8,128)(2,1)S(1)}, bf16[1024,256]{1,0:T(8,128)(2,1)S(1)}, u32[]{:S(2)}, u32[]{:S(2)}) collective-permute-start(bf16[1024,256]{1,0:T(8,128)(2,1)S(1)} %shard_map.48.refs_3_), channel_id=1, source_target_pairs={{0,8},{8,16},{16,24},{24,32},{32,40},{40,48},{48,56},{56,64},{64,7... | collective-permute-start | bytes 1572872 | tf_op jit(solution)/shard_map/ppermute | solution.py:242
  112.0 18.1 %collective-permute-start.8 = (bf16[1024,256]{1,0:T(8,128)(2,1)S(1)}, bf16[1024,256]{1,0:T(8,128)(2,1)S(1)}, u32[]{:S(2)}, u32[]{:S(2)}) collective-permute-start(bf16[1024,256]{1,0:T(8,128)(2,1)S(1)} %shard_map.48.refs_3_), channel_id=1, source_target_pairs={{8,0},{16,8},{24,16},{32,24},{40,32},{48,40},{56,48},{64,56},{72,6... | collective-permute-start | bytes 1572872 | tf_op jit(solution)/shard_map/ppermute | solution.py:243
Sparse Core Ops, SparseCore 0:
  14.3 82.2 all-gather.1

commit v3 on v2

--- a/solution.py
+++ b/solution.py
@@ -132,8 +132,8 @@
     step = TILE // 2
     copies = []
     for i, block in enumerate(refs[:-2]):
-        y = lax.rem(where[2] + turns[i // 2], len(turns))
-        to = pl.ds(pl.multiple_of(y * TILE + i % 2 * step, step), step)
+        y = lax.rem(where[2] + turns[i], len(turns))
+        to = pl.ds(pl.multiple_of(y * step, step), step)
         copy = pltpu.make_async_copy(block, out.at[to, :], done.at[i])
         copy.start()
         copies.append(copy)
@@ -141,8 +141,7 @@
         copy.wait()
 
 
-def order(where, near, far, turns):
-    blocks = [block for pair in zip(near, far) for block in pair]
+def order(where, blocks, turns):
     step, features = blocks[0].shape
     return pl.pallas_call(
         functools.partial(order_kernel, turns),
@@ -157,7 +156,7 @@
 
 
 def project_kernel(*refs):
-    parts, tokens, out = refs[:-2], refs[-2], refs[-1]
+    parts, tokens, out = refs[:-3], refs[-3:-1], refs[-1]
     if len(parts) == 1:
         matrix = parts[0][...]
     else:
@@ -167,21 +166,21 @@
             for h in range(2)
         ]
         matrix = jnp.concatenate(heads, axis=1)
-    step = 512
-    for i in range(0, tokens.shape[0], step):
-        rows = pl.ds(i, step)
-        result = jnp.dot(tokens[rows, :], matrix, preferred_element_type=jnp.float32)
-        out[rows, :] = result.astype(jnp.bfloat16)
+    step = TILE // 2
+    for half, ref in enumerate(tokens):
+        result = jnp.dot(ref[...], matrix, preferred_element_type=jnp.float32).astype(jnp.bfloat16)
+        for y in range(ref.shape[0] // step):
+            out[pl.ds(y * TILE + half * step, step), :] = result[y * step : (y + 1) * step]
 
 
 def project(parts, tokens):
-    rows, features = tokens.shape
+    rows, features = 2 * tokens[0].shape[0], tokens[0].shape[1]
     columns = 2 * HD
     vmem = pl.BlockSpec(memory_space=pltpu.VMEM)
     return pl.pallas_call(
         project_kernel,
         out_shape=jax.ShapeDtypeStruct((rows, columns), jnp.bfloat16),
-        in_specs=[vmem] * (len(parts) + 1),
+        in_specs=[vmem] * (len(parts) + 2),
         out_specs=vmem,
         compiler_params=pltpu.CompilerParams(vmem_limit_bytes=20 * 1024 * 1024),
         cost_estimate=pl.CostEstimate(
@@ -189,7 +188,7 @@
             bytes_accessed=2 * (rows * features + features * columns),
             transcendentals=0,
         ),
-    )(*parts, tokens)
+    )(*parts, *tokens)
 
 
 def body(frames, row_count, video, qkv_weight, window, clips):
@@ -232,7 +231,7 @@
     far = [block_x, along_y(block_x, 1), along_y(block_x, -1), other_x_hi(near[3])]
 
     where = jnp.stack([frame_here // 2 % 2, frame_here % 2, row_here // 2])
-    tokens = order(where, near, far, turns)
+    tokens = [order(where, near, turns), order(where, far, turns)]
     up = [(i, i + 1) for i in range(frames - 1)]
     down = [(j, i) for i, j in up]
     kv, before, after = [], [], []

time: 141 us -> 140 us (level)
  waiting for transfers between devices: 47.8 us -> 37.2 us
  local copies, waits for them, and re-layouts: 9.02 us -> 12.4 us
  blocking collectives: 10.8 us -> 13 us
  starting transfers between devices: 36.6 us -> 38.8 us
  Pallas kernels: 17.6 us -> 19.5 us
    ppermute x7, waiting for transfers between devices: 32.2 us -> 22.5 us  [send(): return lax.ppermute(value, axes, pairs)]
    unnamed x10 -> x18, local copies, waits for them, and re-layouts: 4.2 us -> 7.62 us
    ppermute x7, starting transfers between devices: 26.5 us -> 29 us  [send(): return lax.ppermute(value, axes, pairs)]
    ppermute x2, waiting for transfers between devices: 3.29 us -> 1 us  [body(): before.append(lax.ppermute(result, 'frame', up))]
    all_gather x2, blocking collectives: 4.91 us -> 7.17 us  [body(): lax.all_gather(half, 'frame', axis=0, tiled=True, axis_index_groups=pairs)]
    pallas_call x1 -> x2, Pallas kernels: 2.69 us -> 4.35 us  [order(): pl.pallas_call(functools.partial(order_kernel, turns), out_shape=jax.Shap...]
  transfers between devices with their start and end apart: 12 -> 12, of which waited for: 8 -> 5; matrix products, arithmetic and copies ran while one was open for 2% -> 2% of each run, Pallas kernels for 9% -> 10%
where the time goes in v3:
time: 140 us
  starting transfers between devices  38.8 us (28%)
  waiting for transfers between devices  37.2 us (27%)
  Pallas kernels  19.5 us (14%)
  between operations  16.3 us (12%)
  blocking collectives  13 us (9%)
  local copies, waits for them, and re-layouts  12.4 us (9%)
  other arithmetic  2.51 us (2%)
    ppermute x7, starting transfers between devices, send(): return lax.ppermute(value, axes, pairs)  29 us
    ppermute x7, waiting for transfers between devices, send(): return lax.ppermute(value, axes, pairs)  22.5 us
    all_gather x1, waiting for transfers between devices, body(): lax.all_gather(group, 'frame', axis=0, tiled=True, axis_index_groups=colu...  13.7 us
    pallas_call x3, Pallas kernels, attend(): pl.pallas_call(functools.partial(attend_kernel, heads, frames, state is N...  9.85 us
    unnamed x18, local copies, waits for them, and re-layouts  7.62 us
    all_gather x2, blocking collectives, body(): lax.all_gather(half, 'frame', axis=0, tiled=True, axis_index_groups=pairs)  7.17 us
    all_gather x1, blocking collectives, body(): lax.all_gather(shard, 'frame', axis=0, tiled=True, axis_index_groups=four)  5.88 us
    pallas_call x3, Pallas kernels, project(): pl.pallas_call(project_kernel, out_shape=jax.ShapeDtypeStruct((rows, colu...  5.35 us
  transfers between devices with their start and end apart: 12, of which 5 were waited for; matrix products, arithmetic and copies ran while one was open for 2% of the time, Pallas kernels for 10%

profile of v3, /device:TPU:6, one launch (start us, length us, event | category | flops | bytes accessed | tf_op | source)
XLA Modules:
  0.0 139.8 jit_solution(7825006073823440775)
XLA Ops:
  7.5 5.9 %all_gather.12 = bf16[192,768]{1,0:T(8,128)(2,1)S(1)} all-gather(bf16[48,768]{1,0:T(8,128)(2,1)S(1)} %slice_dynamic-update-slice_fusion), channel_id=1, replica_groups={{0,8,16,24},{32,40,48,56},{64,72,80,88},{96,104,112,120},{128,136,144,1..., dimensions={0}, use_global_device_ids=true | all-gather | bytes 368640 | tf_op jit(solution)/shard_map/all_gather | solution.py:220
  14.1 7.8 %collective-permute-start.3 = (bf16[128,3072]{1,0:T(8,128)(2,1)}, bf16[128,3072]{1,0:T(8,128)(2,1)}, u32[]{:S(2)}, u32[]{:S(2)}) collective-permute-start(bf16[128,3072]{1,0:T(8,128)(2,1)} %bitcast.10), channel_id=1, source_target_pairs={{0,1},{1,0},{2,3},{3,2},{4,5},{5,4},{6,7},{7,6},{8,9},{9,8},{10,11... | collective-permute-start | bytes 2359304 | tf_op jit(solution)/shard_map/ppermute | solution.py:210
  21.9 1.9 %collective-permute-start.2 = (bf16[128,3072]{1,0:T(8,128)(2,1)}, bf16[128,3072]{1,0:T(8,128)(2,1)}, u32[]{:S(2)}, u32[]{:S(2)}) collective-permute-start(bf16[128,3072]{1,0:T(8,128)(2,1)} %bitcast.11), channel_id=1, source_target_pairs={{0,4},{1,5},{2,6},{3,7},{4,0},{5,1},{6,2},{7,3},{8,12},{9,13},{10,... | collective-permute-start | bytes 2359304 | tf_op jit(solution)/shard_map/ppermute | solution.py:210
  23.9 1.9 %collective-permute-start.1 = (bf16[128,3072]{1,0:T(8,128)(2,1)}, bf16[128,3072]{1,0:T(8,128)(2,1)S(1)}, u32[]{:S(2)}, u32[]{:S(2)}) collective-permute-start(bf16[128,3072]{1,0:T(8,128)(2,1)} %bitcast.12), channel_id=1, source_target_pairs={{0,2},{1,3},{2,4},{3,5},{4,6},{5,7},{6,0},{7,1},{8,10},{9,11},{10,... | collective-permute-start | bytes 2359304 | tf_op jit(solution)/shard_map/ppermute | solution.py:210
  25.8 5.1 %collective-permute-start = (bf16[128,3072]{1,0:T(8,128)(2,1)}, bf16[128,3072]{1,0:T(8,128)(2,1)S(1)}, u32[]{:S(2)}, u32[]{:S(2)}) collective-permute-start(bf16[128,3072]{1,0:T(8,128)(2,1)} %bitcast.13), channel_id=1, source_target_pairs={{0,6},{1,7},{2,0},{3,1},{4,2},{5,3},{6,4},{7,5},{8,14},{9,15},{10,... | collective-permute-start | bytes 2359304 | tf_op jit(solution)/shard_map/ppermute | solution.py:210
  30.9 9.3 %collective-permute-done.3.refs_0_ = bf16[128,3072]{1,0:T(8,128)(2,1)} collective-permute-done((bf16[128,3072]{1,0:T(8,128)(2,1)}, bf16[128,3072]{1,0:T(8,128)(2,1)}, u32[]{:S(2)}, u32[]{:S(2)}) %collective-permute-start.3) | collective-permute-done | bytes 786464 | tf_op jit(solution)/shard_map/ppermute | solution.py:210
  40.3 1.9 %collective-permute-start.5 = (bf16[128,3072]{1,0:T(8,128)(2,1)}, bf16[128,3072]{1,0:T(8,128)(2,1)}, u32[]{:S(2)}, u32[]{:S(2)}) collective-permute-start(bf16[128,3072]{1,0:T(8,128)(2,1)} %collective-permute-done.3.refs_0_), channel_id=1, source_target_pairs={{0,2},{1,3},{2,4},{3,5},{4,6},{5,7},{6,0},{7,1},{8,10},{9,11},{10,... | collective-permute-start | bytes 2359304 | tf_op jit(solution)/shard_map/ppermute | solution.py:210
  42.2 5.1 %collective-permute-start.4 = (bf16[128,3072]{1,0:T(8,128)(2,1)}, bf16[128,3072]{1,0:T(8,128)(2,1)}, u32[]{:S(2)}, u32[]{:S(2)}) collective-permute-start(bf16[128,3072]{1,0:T(8,128)(2,1)} %collective-permute-done.3.refs_0_), channel_id=1, source_target_pairs={{0,6},{1,7},{2,0},{3,1},{4,2},{5,3},{6,4},{7,5},{8,14},{9,15},{10,... | collective-permute-start | bytes 2359304 | tf_op jit(solution)/shard_map/ppermute | solution.py:210
  47.4 5.1 %collective-permute-start.6 = (bf16[128,3072]{1,0:T(8,128)(2,1)}, bf16[128,3072]{1,0:T(8,128)(2,1)}, u32[]{:S(2)}, u32[]{:S(2)}) collective-permute-start(bf16[128,3072]{1,0:T(8,128)(2,1)} %collective-permute-done.2.refs_3_), channel_id=1, source_target_pairs={{0,1},{1,0},{2,3},{3,2},{4,5},{5,4},{6,7},{7,6},{8,9},{9,8},{10,11... | collective-permute-start | bytes 2359304 | tf_op jit(solution)/shard_map/ppermute | solution.py:210
  58.5 3.5 %collective-permute-done.1.refs_2_ = bf16[128,3072]{1,0:T(8,128)(2,1)S(1)} collective-permute-done((bf16[128,3072]{1,0:T(8,128)(2,1)}, bf16[128,3072]{1,0:T(8,128)(2,1)S(1)}, u32[]{:S(2)}, u32[]{:S(2)}) %collective-permute-start.1) | collective-permute-done | bytes 786464 | tf_op jit(solution)/shard_map/ppermute | solution.py:210
  63.9 1.1 copy-done.2
  65.0 1.1 copy-done.4
  66.2 1.1 copy-done.6
  67.3 1.9 %shard_map.46.refs_1_.refs_2_ = bf16[512,3072]{1,0:T(8,128)(2,1)S(1)} custom-call(s32[3]{0:T(128)S(1)} %pad_add_fusion.2.where, bf16[128,3072]{1,0:T(8,128)(2,1)S(1)} %bitcast.14, bf16[128,3072]{1,0:T(8,128)(2,1)S(1)} %copy-done.6, bf16[128,3072]{1,0:T(8,128)(2,1)S(1)} %copy-done.4, bf16[128,3072]{1,0:T(8,128)(2,1)} %collective-permute-done.2.refs_3_), custom_call_target="tpu_custom_call" | custom-call | flops 1048576 | bytes 12582912 | tf_op jit(solution)/shard_map/pallas_call | solution.py:146
  69.2 9.7 %collective-permute-done.5.refs_2_ = bf16[128,3072]{1,0:T(8,128)(2,1)} collective-permute-done((bf16[128,3072]{1,0:T(8,128)(2,1)}, bf16[128,3072]{1,0:T(8,128)(2,1)}, u32[]{:S(2)}, u32[]{:S(2)}) %collective-permute-start.5) | collective-permute-done | bytes 786464 | tf_op jit(solution)/shard_map/ppermute | solution.py:210
  78.9 2.4 %shard_map.47.refs_2_.refs_3_ = bf16[512,3072]{1,0:T(8,128)(2,1)S(1)} custom-call(s32[3]{0:T(128)S(1)} %pad_add_fusion.2.where, bf16[128,3072]{1,0:T(8,128)(2,1)} %collective-permute-done.3.refs_0_, bf16[128,3072]{1,0:T(8,128)(2,1)} %collective-permute-done.4.refs_1_, bf16[128,3072]{1,0:T(8,128)(2,1)} %collective-permute-done.5.refs_2_, ...), custom_call_target="tpu_custom_call" | custom-call | flops 1048576 | bytes 12582912 | tf_op jit(solution)/shard_map/pallas_call | solution.py:146
  81.3 1.7 %copy-done = bf16[512,3072]{1,0:T(8,128)(2,1)} copy-done((bf16[512,3072]{1,0:T(8,128)(2,1)}, bf16[512,3072]{1,0:T(8,128)(2,1)S(1)}, u32[]{:S(2)}) %copy-start) | copy-done | bytes 3145752
  83.0 13.7 %all-gather.2.cloned.1.call-done = bf16[3072,640]{1,0:T(8,128)(2,1)} async-done(((bf16[192,640]{1,0:T(8,128)(2,1)}), bf16[3072,640]{1,0:T(8,128)(2,1)}) %all-gather.2.cloned.1.call-update) | async-done | bytes 3932176 | tf_op jit(solution)/shard_map/all_gather | solution.py:223
  96.7 2.3 %fusion.2 = (bf16[3072,256]{1,0:T(8,128)(2,1)S(1)}, bf16[3072,256]{1,0:T(8,128)(2,1)S(1)}) fusion(bf16[3072,640]{1,0:T(8,128)(2,1)} %all-gather.2.cloned.1.call-done), kind=kLoop, calls=%fused_computation.16 | loop fusion | bytes 6291456 | tf_op jit(solution)/shard_map/slice | solution.py:239
  99.5 1.8 %shard_map.48.refs_2_ = bf16[1024,256]{1,0:T(8,128)(2,1)S(1)} custom-call(bf16[3072,256]{1,0:T(8,128)(2,1)S(1)} %get-tuple-element.16.refs_0_, bf16[512,3072]{1,0:T(8,128)(2,1)S(1)} %shard_map.46.refs_1_.refs_2_, bf16[512,3072]{1,0:T(8,128)(2,1)S(1)} %copy-done.1), custom_call_target="tpu_custom_call" | custom-call | flops 1610612736 | bytes 7864320 | tf_op jit(solution)/shard_map/pallas_call | solution.py:180
  101.3 1.9 %collective-permute-start.10 = (bf16[1024,256]{1,0:T(8,128)(2,1)S(1)}, bf16[1024,256]{1,0:T(8,128)(2,1)S(1)}, u32[]{:S(2)}, u32[]{:S(2)}) collective-permute-start(bf16[1024,256]{1,0:T(8,128)(2,1)S(1)} %shard_map.48.refs_2_), channel_id=1, source_target_pairs={{8,0},{16,8},{24,16},{32,24},{40,32},{48,40},{56,48},{64,56},{72,6... | collective-permute-start | bytes 1572872 | tf_op jit(solution)/shard_map/ppermute | solution.py:242
  103.2 2.4 %collective-permute-start.9 = (bf16[1024,256]{1,0:T(8,128)(2,1)S(1)}, bf16[1024,256]{1,0:T(8,128)(2,1)S(1)}, u32[]{:S(2)}, u32[]{:S(2)}) collective-permute-start(bf16[1024,256]{1,0:T(8,128)(2,1)S(1)} %shard_map.48.refs_2_), channel_id=1, source_target_pairs={{0,8},{8,16},{16,24},{24,32},{32,40},{40,48},{48,56},{56,64},{64,7... | collective-permute-start | bytes 1572872 | tf_op jit(solution)/shard_map/ppermute | solution.py:241
  105.7 1.8 %shard_map.49.refs_3_ = bf16[1024,256]{1,0:T(8,128)(2,1)S(1)} custom-call(bf16[3072,256]{1,0:T(8,128)(2,1)S(1)} %get-tuple-element.15.refs_0_, bf16[512,3072]{1,0:T(8,128)(2,1)S(1)} %shard_map.46.refs_1_.refs_2_, bf16[512,3072]{1,0:T(8,128)(2,1)S(1)} %copy-done.1), custom_call_target="tpu_custom_call" | custom-call | flops 1610612736 | bytes 7864320 | tf_op jit(solution)/shard_map/pallas_call | solution.py:180
  107.5 3.3 %collective-permute-start.8 = (bf16[1024,256]{1,0:T(8,128)(2,1)S(1)}, bf16[1024,256]{1,0:T(8,128)(2,1)S(1)}, u32[]{:S(2)}, u32[]{:S(2)}) collective-permute-start(bf16[1024,256]{1,0:T(8,128)(2,1)S(1)} %shard_map.49.refs_3_), channel_id=1, source_target_pairs={{8,0},{16,8},{24,16},{32,24},{40,32},{48,40},{56,48},{64,56},{72,6... | collective-permute-start | bytes 1572872 | tf_op jit(solution)/shard_map/ppermute | solution.py:242
  110.8 2.2 %collective-permute-start.7 = (bf16[1024,256]{1,0:T(8,128)(2,1)S(1)}, bf16[1024,256]{1,0:T(8,128)(2,1)S(1)}, u32[]{:S(2)}, u32[]{:S(2)}) collective-permute-start(bf16[1024,256]{1,0:T(8,128)(2,1)S(1)} %shard_map.49.refs_3_), channel_id=1, source_target_pairs={{0,8},{8,16},{16,24},{24,32},{32,40},{40,48},{48,56},{56,64},{64,7... | collective-permute-start | bytes 1572872 | tf_op jit(solution)/shard_map/ppermute | solution.py:241
  113.1 4.6 %all_gather.15.refs_1_ = bf16[3072,128]{1,0:T(8,128)(2,1)S(1)} all-gather(bf16[1536,128]{1,0:T(8,128)(2,1)S(1)} %get-tuple-element.17), channel_id=1, replica_groups={{0,8},{16,24},{32,40},{48,56},{64,72},{80,88},{96,104},{112,120},{128,1..., dimensions={0}, use_global_device_ids=true | all-gather | bytes 1179648 | tf_op jit(solution)/shard_map/all_gather | solution.py:246
  117.7 2.5 %all_gather.14.refs_0_ = bf16[3072,128]{1,0:T(8,128)(2,1)S(1)} all-gather(bf16[1536,128]{1,0:T(8,128)(2,1)S(1)} %get-tuple-element.18), channel_id=1, replica_groups={{0,8},{16,24},{32,40},{48,56},{64,72},{80,88},{96,104},{112,120},{128,1..., dimensions={0}, use_global_device_ids=true | all-gather | bytes 1179648 | tf_op jit(solution)/shard_map/all_gather | solution.py:246
  120.2 1.8 %shard_map.50.refs_1_ = bf16[1024,256]{1,0:T(8,128)(2,1)S(1)} custom-call(bf16[3072,128]{1,0:T(8,128)(2,1)S(1)} %all_gather.14.refs_0_, bf16[3072,128]{1,0:T(8,128)(2,1)S(1)} %all_gather.15.refs_1_, bf16[512,3072]{1,0:T(8,128)(2,1)S(1)} %shard_map.46.refs_1_.refs_2_, bf16[512,3072]{1,0:T(8,128)(2,1)S(1)} %copy-done.1), custom_call_target="tpu_custom_call" | custom-call | flops 1610612736 | bytes 7864320 | tf_op jit(solution)/shard_map/pallas_call | solution.py:180
  122.0 3.1 %shard_map.51 = (f32[1024,512]{1,0:T(8,128)S(1)}, f32[1024,128]{1,0:T(8,128)S(1)}) custom-call(s32[9]{0:T(128)S(1)} %pad_add_fusion.3.refs_0_, bf16[1024,256]{1,0:T(8,128)(2,1)S(1)} %shard_map.50.refs_1_, bf16[1024,256]{1,0:T(8,128)(2,1)S(1)} %shard_map.48.refs_2_, bf16[1024,256]{1,0:T(8,128)(2,1)S(1)} %shard_map.49.refs_3_), custom_call_target="tpu_custom_call" | custom-call | flops 1342177280 | bytes 2097152 | tf_op jit(solution)/shard_map/pallas_call | solution.py:118
  125.2 3.0 %shard_map.52.refs_6_ = bf16[1024,128]{1,0:T(8,128)(2,1)S(1)} custom-call(s32[11]{0:T(128)S(1)} %pad_add_fusion.1.refs_0_, bf16[1024,256]{1,0:T(8,128)(2,1)S(1)} %shard_map.50.refs_1_, bf16[1024,256]{1,0:T(8,128)(2,1)S(1)} %collective-permute-done.9.refs_2_, bf16[1024,256]{1,0:T(8,128)(2,1)S(1)} %collective-permute-done.10.refs_3_, ...), custom_call_target="tpu_custom_call" | custom-call | flops 1342177280 | bytes 2621440 | tf_op jit(solution)/shard_map/pallas_call | solution.py:118
  128.2 1.0 collective-permute-done.7.refs_2_
  129.2 3.7 %shard_map.53 = bf16[1024,256]{1,0:T(8,128)(2,1)} custom-call(s32[11]{0:T(128)S(1)} %pad_add_fusion.1.refs_0_, bf16[1024,256]{1,0:T(8,128)(2,1)S(1)} %shard_map.50.refs_1_, bf16[1024,256]{1,0:T(8,128)(2,1)S(1)} %collective-permute-done.7.refs_2_, bf16[1024,256]{1,0:T(8,128)(2,1)S(1)} %collective-permute-done.8.refs_3_, ...), custom_call_target="tpu_custom_call" | custom-call | flops 1342177280 | bytes 2621440 | tf_op jit(solution)/shard_map/pallas_call | solution.py:118
  (41 shorter events, 7.6 us)
Async XLA Ops:
  6.5 90.1 %all-gather.2.cloned.1.call-start = ((), (), s32[]{:S(2)}) async-start(), calls=%async_computation | async-start | bytes 4177920 | tf_op jit(solution)/shard_map/all_gather | solution.py:223
  14.1 26.1 %collective-permute-start.3 = (bf16[128,3072]{1,0:T(8,128)(2,1)}, bf16[128,3072]{1,0:T(8,128)(2,1)}, u32[]{:S(2)}, u32[]{:S(2)}) collective-permute-start(bf16[128,3072]{1,0:T(8,128)(2,1)} %bitcast.10), channel_id=1, source_target_pairs={{0,1},{1,0},{2,3},{3,2},{4,5},{5,4},{6,7},{7,6},{8,9},{9,8},{10,11... | collective-permute-start | bytes 2359304 | tf_op jit(solution)/shard_map/ppermute | solution.py:210
  21.9 25.4 %collective-permute-start.2 = (bf16[128,3072]{1,0:T(8,128)(2,1)}, bf16[128,3072]{1,0:T(8,128)(2,1)}, u32[]{:S(2)}, u32[]{:S(2)}) collective-permute-start(bf16[128,3072]{1,0:T(8,128)(2,1)} %bitcast.11), channel_id=1, source_target_pairs={{0,4},{1,5},{2,6},{3,7},{4,0},{5,1},{6,2},{7,3},{8,12},{9,13},{10,... | collective-permute-start | bytes 2359304 | tf_op jit(solution)/shard_map/ppermute | solution.py:210
  23.9 38.1 %collective-permute-start.1 = (bf16[128,3072]{1,0:T(8,128)(2,1)}, bf16[128,3072]{1,0:T(8,128)(2,1)S(1)}, u32[]{:S(2)}, u32[]{:S(2)}) collective-permute-start(bf16[128,3072]{1,0:T(8,128)(2,1)} %bitcast.12), channel_id=1, source_target_pairs={{0,2},{1,3},{2,4},{3,5},{4,6},{5,7},{6,0},{7,1},{8,10},{9,11},{10,... | collective-permute-start | bytes 2359304 | tf_op jit(solution)/shard_map/ppermute | solution.py:210
  25.8 37.1 %collective-permute-start = (bf16[128,3072]{1,0:T(8,128)(2,1)}, bf16[128,3072]{1,0:T(8,128)(2,1)S(1)}, u32[]{:S(2)}, u32[]{:S(2)}) collective-permute-start(bf16[128,3072]{1,0:T(8,128)(2,1)} %bitcast.13), channel_id=1, source_target_pairs={{0,6},{1,7},{2,0},{3,1},{4,2},{5,3},{6,4},{7,5},{8,14},{9,15},{10,... | collective-permute-start | bytes 2359304 | tf_op jit(solution)/shard_map/ppermute | solution.py:210
  40.3 38.6 %collective-permute-start.5 = (bf16[128,3072]{1,0:T(8,128)(2,1)}, bf16[128,3072]{1,0:T(8,128)(2,1)}, u32[]{:S(2)}, u32[]{:S(2)}) collective-permute-start(bf16[128,3072]{1,0:T(8,128)(2,1)} %collective-permute-done.3.refs_0_), channel_id=1, source_target_pairs={{0,2},{1,3},{2,4},{3,5},{4,6},{5,7},{6,0},{7,1},{8,10},{9,11},{10,... | collective-permute-start | bytes 2359304 | tf_op jit(solution)/shard_map/ppermute | solution.py:210
  42.2 36.7 %collective-permute-start.4 = (bf16[128,3072]{1,0:T(8,128)(2,1)}, bf16[128,3072]{1,0:T(8,128)(2,1)}, u32[]{:S(2)}, u32[]{:S(2)}) collective-permute-start(bf16[128,3072]{1,0:T(8,128)(2,1)} %collective-permute-done.3.refs_0_), channel_id=1, source_target_pairs={{0,6},{1,7},{2,0},{3,1},{4,2},{5,3},{6,4},{7,5},{8,14},{9,15},{10,... | collective-permute-start | bytes 2359304 | tf_op jit(solution)/shard_map/ppermute | solution.py:210
  47.4 31.5 %collective-permute-start.6 = (bf16[128,3072]{1,0:T(8,128)(2,1)}, bf16[128,3072]{1,0:T(8,128)(2,1)}, u32[]{:S(2)}, u32[]{:S(2)}) collective-permute-start(bf16[128,3072]{1,0:T(8,128)(2,1)} %collective-permute-done.2.refs_3_), channel_id=1, source_target_pairs={{0,1},{1,0},{2,3},{3,2},{4,5},{5,4},{6,7},{7,6},{8,9},{9,8},{10,11... | collective-permute-start | bytes 2359304 | tf_op jit(solution)/shard_map/ppermute | solution.py:210
  62.0 0.9 copy-start.3
  62.9 0.9 copy-start.5
  63.9 1.1 copy-start.2
  65.0 1.1 copy-start.4
  66.2 1.1 copy-start.6
  81.3 1.7 %copy-start = (bf16[512,3072]{1,0:T(8,128)(2,1)}, bf16[512,3072]{1,0:T(8,128)(2,1)S(1)}, u32[]{:S(2)}) copy-start(bf16[512,3072]{1,0:T(8,128)(2,1)S(1)} %shard_map.47.refs_2_.refs_3_) | copy-start | bytes 9437188
  96.7 2.9 %copy-start.1 = (bf16[512,3072]{1,0:T(8,128)(2,1)S(1)}, bf16[512,3072]{1,0:T(8,128)(2,1)}, u32[]{:S(2)}) copy-start(bf16[512,3072]{1,0:T(8,128)(2,1)} %copy-done) | copy-start | bytes 9437188
  101.3 23.8 %collective-permute-start.10 = (bf16[1024,256]{1,0:T(8,128)(2,1)S(1)}, bf16[1024,256]{1,0:T(8,128)(2,1)S(1)}, u32[]{:S(2)}, u32[]{:S(2)}) collective-permute-start(bf16[1024,256]{1,0:T(8,128)(2,1)S(1)} %shard_map.48.refs_2_), channel_id=1, source_target_pairs={{8,0},{16,8},{24,16},{32,24},{40,32},{48,40},{56,48},{64,56},{72,6... | collective-permute-start | bytes 1572872 | tf_op jit(solution)/shard_map/ppermute | solution.py:242
  103.2 21.9 %collective-permute-start.9 = (bf16[1024,256]{1,0:T(8,128)(2,1)S(1)}, bf16[1024,256]{1,0:T(8,128)(2,1)S(1)}, u32[]{:S(2)}, u32[]{:S(2)}) collective-permute-start(bf16[1024,256]{1,0:T(8,128)(2,1)S(1)} %shard_map.48.refs_2_), channel_id=1, source_target_pairs={{0,8},{8,16},{16,24},{24,32},{32,40},{40,48},{48,56},{56,64},{64,7... | collective-permute-start | bytes 1572872 | tf_op jit(solution)/shard_map/ppermute | solution.py:241
  107.5 5.5 %slice-start = ((bf16[3072,640]{1,0:T(8,128)(2,1)}), bf16[3072,128]{1,0:T(8,128)(2,1)S(1)}, s32[]{:S(2)}) async-start(bf16[3072,640]{1,0:T(8,128)(2,1)} %all-gather.2.cloned.1.call-done), calls=%async_computation.1 | async-start | bytes 1572864 | tf_op jit(solution)/shard_map/slice | solution.py:243
  107.5 20.7 %collective-permute-start.8 = (bf16[1024,256]{1,0:T(8,128)(2,1)S(1)}, bf16[1024,256]{1,0:T(8,128)(2,1)S(1)}, u32[]{:S(2)}, u32[]{:S(2)}) collective-permute-start(bf16[1024,256]{1,0:T(8,128)(2,1)S(1)} %shard_map.49.refs_3_), channel_id=1, source_target_pairs={{8,0},{16,8},{24,16},{32,24},{40,32},{48,40},{56,48},{64,56},{72,6... | collective-permute-start | bytes 1572872 | tf_op jit(solution)/shard_map/ppermute | solution.py:242
  110.8 18.4 %collective-permute-start.7 = (bf16[1024,256]{1,0:T(8,128)(2,1)S(1)}, bf16[1024,256]{1,0:T(8,128)(2,1)S(1)}, u32[]{:S(2)}, u32[]{:S(2)}) collective-permute-start(bf16[1024,256]{1,0:T(8,128)(2,1)S(1)} %shard_map.49.refs_3_), channel_id=1, source_target_pairs={{0,8},{8,16},{16,24},{24,32},{32,40},{40,48},{48,56},{56,64},{64,7... | collective-permute-start | bytes 1572872 | tf_op jit(solution)/shard_map/ppermute | solution.py:241
Sparse Core Ops, SparseCore 0:
  14.3 82.3 all-gather.1

commit v4 on v3

--- a/solution.py
+++ b/solution.py
@@ -215,11 +215,10 @@
     four = [[g * GROUP + i for i in range(GROUP)] for g in range(depth)]
 
     shard = qkv_weight.reshape(share, 3 * width)
-    cut = lambda j, h: shard[:, j * width + h * HD : j * width + (h + 1) * HD]
-    shard = jnp.concatenate([cut(1, 0), cut(2, 0), cut(1, 1), cut(2, 1), shard[:, :width]], axis=1)
     group = lax.all_gather(shard, "frame", axis=0, tiled=True, axis_index_groups=four)
-    mine = lax.dynamic_slice_in_dim(group, 4 * HD + frame_here % 2 * HD, HD, 1)
-    group = jnp.concatenate([group[:, : 4 * HD], mine], axis=1)
+    cut = lambda j, h: group[:, j * width + h * HD : j * width + (h + 1) * HD]
+    mine = lax.dynamic_slice_in_dim(group, frame_here % 2 * HD, HD, 1)
+    group = jnp.concatenate([cut(1, 0), cut(2, 0), cut(1, 1), cut(2, 1), mine], axis=1)
     matrix = lax.all_gather(group, "frame", axis=0, tiled=True, axis_index_groups=columns)
 
     block = video.reshape(-1, features)

time: 140 us -> 140 us (level)
    unnamed x18 -> x20, local copies, waits for them, and re-layouts: 7.62 us -> 8.33 us
where the time goes in v4:
time: 140 us
  starting transfers between devices  38.8 us (28%)
  waiting for transfers between devices  37.4 us (27%)
  Pallas kernels  19.6 us (14%)
  between operations  16.1 us (12%)
  local copies, waits for them, and re-layouts  13 us (9%)
  blocking collectives  13 us (9%)
  other arithmetic  1.79 us (1%)
    ppermute x7, starting transfers between devices, send(): return lax.ppermute(value, axes, pairs)  29 us
    ppermute x7, waiting for transfers between devices, send(): return lax.ppermute(value, axes, pairs)  22.7 us
    all_gather x1, waiting for transfers between devices, body(): lax.all_gather(group, 'frame', axis=0, tiled=True, axis_index_groups=colu...  13.6 us
    pallas_call x3, Pallas kernels, attend(): pl.pallas_call(functools.partial(attend_kernel, heads, frames, state is N...  9.85 us
    unnamed x20, local copies, waits for them, and re-layouts  8.33 us
    all_gather x2, blocking collectives, body(): lax.all_gather(half, 'frame', axis=0, tiled=True, axis_index_groups=pairs)  7.17 us
    all_gather x1, blocking collectives, body(): lax.all_gather(shard, 'frame', axis=0, tiled=True, axis_index_groups=four)  5.86 us
    pallas_call x3, Pallas kernels, project(): pl.pallas_call(project_kernel, out_shape=jax.ShapeDtypeStruct((rows, colu...  5.36 us
  transfers between devices with their start and end apart: 12, of which 5 were waited for; matrix products, arithmetic and copies ran while one was open for 2% of the time, Pallas kernels for 10%

profile of v4, /device:TPU:6, one launch (start us, length us, event | category | flops | bytes accessed | tf_op | source)
XLA Modules:
  0.0 139.7 jit_solution(10394860061126548162)
XLA Ops:
  7.4 5.9 %all_gather.12 = bf16[192,768]{1,0:T(8,128)(2,1)S(1)} all-gather(bf16[48,768]{1,0:T(8,128)(2,1)S(1)} %bitcast.15), channel_id=1, replica_groups={{0,8,16,24},{32,40,48,56},{64,72,80,88},{96,104,112,120},{128,136,144,1..., dimensions={0}, use_global_device_ids=true | all-gather | bytes 368640 | tf_op jit(solution)/shard_map/all_gather | solution.py:218
  14.1 7.8 %collective-permute-start.3 = (bf16[128,3072]{1,0:T(8,128)(2,1)}, bf16[128,3072]{1,0:T(8,128)(2,1)}, u32[]{:S(2)}, u32[]{:S(2)}) collective-permute-start(bf16[128,3072]{1,0:T(8,128)(2,1)} %bitcast.10), channel_id=1, source_target_pairs={{0,1},{1,0},{2,3},{3,2},{4,5},{5,4},{6,7},{7,6},{8,9},{9,8},{10,11... | collective-permute-start | bytes 2359304 | tf_op jit(solution)/shard_map/ppermute | solution.py:210
  21.9 1.9 %collective-permute-start.2 = (bf16[128,3072]{1,0:T(8,128)(2,1)}, bf16[128,3072]{1,0:T(8,128)(2,1)}, u32[]{:S(2)}, u32[]{:S(2)}) collective-permute-start(bf16[128,3072]{1,0:T(8,128)(2,1)} %bitcast.11), channel_id=1, source_target_pairs={{0,4},{1,5},{2,6},{3,7},{4,0},{5,1},{6,2},{7,3},{8,12},{9,13},{10,... | collective-permute-start | bytes 2359304 | tf_op jit(solution)/shard_map/ppermute | solution.py:210
  23.8 1.9 %collective-permute-start.1 = (bf16[128,3072]{1,0:T(8,128)(2,1)}, bf16[128,3072]{1,0:T(8,128)(2,1)S(1)}, u32[]{:S(2)}, u32[]{:S(2)}) collective-permute-start(bf16[128,3072]{1,0:T(8,128)(2,1)} %bitcast.12), channel_id=1, source_target_pairs={{0,2},{1,3},{2,4},{3,5},{4,6},{5,7},{6,0},{7,1},{8,10},{9,11},{10,... | collective-permute-start | bytes 2359304 | tf_op jit(solution)/shard_map/ppermute | solution.py:210
  25.8 5.1 %collective-permute-start = (bf16[128,3072]{1,0:T(8,128)(2,1)}, bf16[128,3072]{1,0:T(8,128)(2,1)S(1)}, u32[]{:S(2)}, u32[]{:S(2)}) collective-permute-start(bf16[128,3072]{1,0:T(8,128)(2,1)} %bitcast.13), channel_id=1, source_target_pairs={{0,6},{1,7},{2,0},{3,1},{4,2},{5,3},{6,4},{7,5},{8,14},{9,15},{10,... | collective-permute-start | bytes 2359304 | tf_op jit(solution)/shard_map/ppermute | solution.py:210
  30.9 9.3 %collective-permute-done.3.refs_0_ = bf16[128,3072]{1,0:T(8,128)(2,1)} collective-permute-done((bf16[128,3072]{1,0:T(8,128)(2,1)}, bf16[128,3072]{1,0:T(8,128)(2,1)}, u32[]{:S(2)}, u32[]{:S(2)}) %collective-permute-start.3) | collective-permute-done | bytes 786464 | tf_op jit(solution)/shard_map/ppermute | solution.py:210
  40.3 1.9 %collective-permute-start.5 = (bf16[128,3072]{1,0:T(8,128)(2,1)}, bf16[128,3072]{1,0:T(8,128)(2,1)}, u32[]{:S(2)}, u32[]{:S(2)}) collective-permute-start(bf16[128,3072]{1,0:T(8,128)(2,1)} %collective-permute-done.3.refs_0_), channel_id=1, source_target_pairs={{0,2},{1,3},{2,4},{3,5},{4,6},{5,7},{6,0},{7,1},{8,10},{9,11},{10,... | collective-permute-start | bytes 2359304 | tf_op jit(solution)/shard_map/ppermute | solution.py:210
  42.2 5.1 %collective-permute-start.4 = (bf16[128,3072]{1,0:T(8,128)(2,1)}, bf16[128,3072]{1,0:T(8,128)(2,1)}, u32[]{:S(2)}, u32[]{:S(2)}) collective-permute-start(bf16[128,3072]{1,0:T(8,128)(2,1)} %collective-permute-done.3.refs_0_), channel_id=1, source_target_pairs={{0,6},{1,7},{2,0},{3,1},{4,2},{5,3},{6,4},{7,5},{8,14},{9,15},{10,... | collective-permute-start | bytes 2359304 | tf_op jit(solution)/shard_map/ppermute | solution.py:210
  47.3 5.1 %collective-permute-start.6 = (bf16[128,3072]{1,0:T(8,128)(2,1)}, bf16[128,3072]{1,0:T(8,128)(2,1)}, u32[]{:S(2)}, u32[]{:S(2)}) collective-permute-start(bf16[128,3072]{1,0:T(8,128)(2,1)} %collective-permute-done.2.refs_3_), channel_id=1, source_target_pairs={{0,1},{1,0},{2,3},{3,2},{4,5},{5,4},{6,7},{7,6},{8,9},{9,8},{10,11... | collective-permute-start | bytes 2359304 | tf_op jit(solution)/shard_map/ppermute | solution.py:210
  58.3 3.7 %collective-permute-done.1.refs_2_ = bf16[128,3072]{1,0:T(8,128)(2,1)S(1)} collective-permute-done((bf16[128,3072]{1,0:T(8,128)(2,1)}, bf16[128,3072]{1,0:T(8,128)(2,1)S(1)}, u32[]{:S(2)}, u32[]{:S(2)}) %collective-permute-start.1) | collective-permute-done | bytes 786464 | tf_op jit(solution)/shard_map/ppermute | solution.py:210
  63.9 1.1 copy-done.2
  65.0 1.1 copy-done.4
  66.1 1.1 copy-done.6
  67.3 1.9 %shard_map.46.refs_1_.refs_2_ = bf16[512,3072]{1,0:T(8,128)(2,1)S(1)} custom-call(s32[3]{0:T(128)S(1)} %pad_add_fusion.2.where, bf16[128,3072]{1,0:T(8,128)(2,1)S(1)} %bitcast.14, bf16[128,3072]{1,0:T(8,128)(2,1)S(1)} %copy-done.6, bf16[128,3072]{1,0:T(8,128)(2,1)S(1)} %copy-done.4, bf16[128,3072]{1,0:T(8,128)(2,1)} %collective-permute-done.2.refs_3_), custom_call_target="tpu_custom_call" | custom-call | flops 1048576 | bytes 12582912 | tf_op jit(solution)/shard_map/pallas_call | solution.py:146
  69.2 9.7 %collective-permute-done.5.refs_2_ = bf16[128,3072]{1,0:T(8,128)(2,1)} collective-permute-done((bf16[128,3072]{1,0:T(8,128)(2,1)}, bf16[128,3072]{1,0:T(8,128)(2,1)}, u32[]{:S(2)}, u32[]{:S(2)}) %collective-permute-start.5) | collective-permute-done | bytes 786464 | tf_op jit(solution)/shard_map/ppermute | solution.py:210
  78.9 2.4 %shard_map.47.refs_2_.refs_3_ = bf16[512,3072]{1,0:T(8,128)(2,1)S(1)} custom-call(s32[3]{0:T(128)S(1)} %pad_add_fusion.2.where, bf16[128,3072]{1,0:T(8,128)(2,1)} %collective-permute-done.3.refs_0_, bf16[128,3072]{1,0:T(8,128)(2,1)} %collective-permute-done.4.refs_1_, bf16[128,3072]{1,0:T(8,128)(2,1)} %collective-permute-done.5.refs_2_, ...), custom_call_target="tpu_custom_call" | custom-call | flops 1048576 | bytes 12582912 | tf_op jit(solution)/shard_map/pallas_call | solution.py:146
  81.3 1.7 %copy-done = bf16[512,3072]{1,0:T(8,128)(2,1)} copy-done((bf16[512,3072]{1,0:T(8,128)(2,1)}, bf16[512,3072]{1,0:T(8,128)(2,1)S(1)}, u32[]{:S(2)}) %copy-start) | copy-done | bytes 3145752
  83.0 13.6 %all-gather.2.cloned.1.call-done = bf16[3072,640]{1,0:T(8,128)(2,1)} async-done(((bf16[192,640]{1,0:T(8,128)(2,1)}), bf16[3072,640]{1,0:T(8,128)(2,1)}) %all-gather.2.cloned.1.call-update) | async-done | bytes 3932176 | tf_op jit(solution)/shard_map/all_gather | solution.py:222
  96.6 2.3 %fusion.2 = (bf16[3072,256]{1,0:T(8,128)(2,1)S(1)}, bf16[3072,256]{1,0:T(8,128)(2,1)S(1)}) fusion(bf16[3072,640]{1,0:T(8,128)(2,1)} %all-gather.2.cloned.1.call-done), kind=kLoop, calls=%fused_computation.14 | loop fusion | bytes 6291456 | tf_op jit(solution)/shard_map/slice | solution.py:238
  99.5 1.8 %shard_map.48.refs_2_ = bf16[1024,256]{1,0:T(8,128)(2,1)S(1)} custom-call(bf16[3072,256]{1,0:T(8,128)(2,1)S(1)} %get-tuple-element.16.refs_0_, bf16[512,3072]{1,0:T(8,128)(2,1)S(1)} %shard_map.46.refs_1_.refs_2_, bf16[512,3072]{1,0:T(8,128)(2,1)S(1)} %copy-done.1), custom_call_target="tpu_custom_call" | custom-call | flops 1610612736 | bytes 7864320 | tf_op jit(solution)/shard_map/pallas_call | solution.py:180
  101.3 1.9 %collective-permute-start.10 = (bf16[1024,256]{1,0:T(8,128)(2,1)S(1)}, bf16[1024,256]{1,0:T(8,128)(2,1)S(1)}, u32[]{:S(2)}, u32[]{:S(2)}) collective-permute-start(bf16[1024,256]{1,0:T(8,128)(2,1)S(1)} %shard_map.48.refs_2_), channel_id=1, source_target_pairs={{8,0},{16,8},{24,16},{32,24},{40,32},{48,40},{56,48},{64,56},{72,6... | collective-permute-start | bytes 1572872 | tf_op jit(solution)/shard_map/ppermute | solution.py:241
  103.2 2.4 %collective-permute-start.9 = (bf16[1024,256]{1,0:T(8,128)(2,1)S(1)}, bf16[1024,256]{1,0:T(8,128)(2,1)S(1)}, u32[]{:S(2)}, u32[]{:S(2)}) collective-permute-start(bf16[1024,256]{1,0:T(8,128)(2,1)S(1)} %shard_map.48.refs_2_), channel_id=1, source_target_pairs={{0,8},{8,16},{16,24},{24,32},{32,40},{40,48},{48,56},{56,64},{64,7... | collective-permute-start | bytes 1572872 | tf_op jit(solution)/shard_map/ppermute | solution.py:240
  105.6 1.8 %shard_map.49.refs_3_ = bf16[1024,256]{1,0:T(8,128)(2,1)S(1)} custom-call(bf16[3072,256]{1,0:T(8,128)(2,1)S(1)} %get-tuple-element.15.refs_0_, bf16[512,3072]{1,0:T(8,128)(2,1)S(1)} %shard_map.46.refs_1_.refs_2_, bf16[512,3072]{1,0:T(8,128)(2,1)S(1)} %copy-done.1), custom_call_target="tpu_custom_call" | custom-call | flops 1610612736 | bytes 7864320 | tf_op jit(solution)/shard_map/pallas_call | solution.py:180
  107.4 3.3 %collective-permute-start.8 = (bf16[1024,256]{1,0:T(8,128)(2,1)S(1)}, bf16[1024,256]{1,0:T(8,128)(2,1)S(1)}, u32[]{:S(2)}, u32[]{:S(2)}) collective-permute-start(bf16[1024,256]{1,0:T(8,128)(2,1)S(1)} %shard_map.49.refs_3_), channel_id=1, source_target_pairs={{8,0},{16,8},{24,16},{32,24},{40,32},{48,40},{56,48},{64,56},{72,6... | collective-permute-start | bytes 1572872 | tf_op jit(solution)/shard_map/ppermute | solution.py:241
  110.7 2.2 %collective-permute-start.7 = (bf16[1024,256]{1,0:T(8,128)(2,1)S(1)}, bf16[1024,256]{1,0:T(8,128)(2,1)S(1)}, u32[]{:S(2)}, u32[]{:S(2)}) collective-permute-start(bf16[1024,256]{1,0:T(8,128)(2,1)S(1)} %shard_map.49.refs_3_), channel_id=1, source_target_pairs={{0,8},{8,16},{16,24},{24,32},{32,40},{40,48},{48,56},{56,64},{64,7... | collective-permute-start | bytes 1572872 | tf_op jit(solution)/shard_map/ppermute | solution.py:240
  113.0 4.6 %all_gather.15.refs_1_ = bf16[3072,128]{1,0:T(8,128)(2,1)S(1)} all-gather(bf16[1536,128]{1,0:T(8,128)(2,1)S(1)} %get-tuple-element.17), channel_id=1, replica_groups={{0,8},{16,24},{32,40},{48,56},{64,72},{80,88},{96,104},{112,120},{128,1..., dimensions={0}, use_global_device_ids=true | all-gather | bytes 1179648 | tf_op jit(solution)/shard_map/all_gather | solution.py:245
  117.7 2.5 %all_gather.14.refs_0_ = bf16[3072,128]{1,0:T(8,128)(2,1)S(1)} all-gather(bf16[1536,128]{1,0:T(8,128)(2,1)S(1)} %get-tuple-element.18), channel_id=1, replica_groups={{0,8},{16,24},{32,40},{48,56},{64,72},{80,88},{96,104},{112,120},{128,1..., dimensions={0}, use_global_device_ids=true | all-gather | bytes 1179648 | tf_op jit(solution)/shard_map/all_gather | solution.py:245
  120.2 1.8 %shard_map.50.refs_1_ = bf16[1024,256]{1,0:T(8,128)(2,1)S(1)} custom-call(bf16[3072,128]{1,0:T(8,128)(2,1)S(1)} %all_gather.14.refs_0_, bf16[3072,128]{1,0:T(8,128)(2,1)S(1)} %all_gather.15.refs_1_, bf16[512,3072]{1,0:T(8,128)(2,1)S(1)} %shard_map.46.refs_1_.refs_2_, bf16[512,3072]{1,0:T(8,128)(2,1)S(1)} %copy-done.1), custom_call_target="tpu_custom_call" | custom-call | flops 1610612736 | bytes 7864320 | tf_op jit(solution)/shard_map/pallas_call | solution.py:180
  122.0 3.1 %shard_map.51 = (f32[1024,512]{1,0:T(8,128)S(1)}, f32[1024,128]{1,0:T(8,128)S(1)}) custom-call(s32[9]{0:T(128)S(1)} %pad_add_fusion.3.refs_0_, bf16[1024,256]{1,0:T(8,128)(2,1)S(1)} %shard_map.50.refs_1_, bf16[1024,256]{1,0:T(8,128)(2,1)S(1)} %shard_map.48.refs_2_, bf16[1024,256]{1,0:T(8,128)(2,1)S(1)} %shard_map.49.refs_3_), custom_call_target="tpu_custom_call" | custom-call | flops 1342177280 | bytes 2097152 | tf_op jit(solution)/shard_map/pallas_call | solution.py:118
  125.1 3.0 %shard_map.52.refs_6_ = bf16[1024,128]{1,0:T(8,128)(2,1)S(1)} custom-call(s32[11]{0:T(128)S(1)} %pad_add_fusion.1.refs_0_, bf16[1024,256]{1,0:T(8,128)(2,1)S(1)} %shard_map.50.refs_1_, bf16[1024,256]{1,0:T(8,128)(2,1)S(1)} %collective-permute-done.9.refs_2_, bf16[1024,256]{1,0:T(8,128)(2,1)S(1)} %collective-permute-done.10.refs_3_, ...), custom_call_target="tpu_custom_call" | custom-call | flops 1342177280 | bytes 2621440 | tf_op jit(solution)/shard_map/pallas_call | solution.py:118
  128.1 1.0 collective-permute-done.7.refs_2_
  129.1 3.7 %shard_map.53 = bf16[1024,256]{1,0:T(8,128)(2,1)} custom-call(s32[11]{0:T(128)S(1)} %pad_add_fusion.1.refs_0_, bf16[1024,256]{1,0:T(8,128)(2,1)S(1)} %shard_map.50.refs_1_, bf16[1024,256]{1,0:T(8,128)(2,1)S(1)} %collective-permute-done.7.refs_2_, bf16[1024,256]{1,0:T(8,128)(2,1)S(1)} %collective-permute-done.8.refs_3_, ...), custom_call_target="tpu_custom_call" | custom-call | flops 1342177280 | bytes 2621440 | tf_op jit(solution)/shard_map/pallas_call | solution.py:118
  (40 shorter events, 7.5 us)
Async XLA Ops:
  6.5 90.1 %all-gather.2.cloned.1.call-start = ((), (), s32[]{:S(2)}) async-start(), calls=%async_computation | async-start | bytes 4177920 | tf_op jit(solution)/shard_map/all_gather | solution.py:222
  13.4 0.7 copy-start.7
  14.1 26.1 %collective-permute-start.3 = (bf16[128,3072]{1,0:T(8,128)(2,1)}, bf16[128,3072]{1,0:T(8,128)(2,1)}, u32[]{:S(2)}, u32[]{:S(2)}) collective-permute-start(bf16[128,3072]{1,0:T(8,128)(2,1)} %bitcast.10), channel_id=1, source_target_pairs={{0,1},{1,0},{2,3},{3,2},{4,5},{5,4},{6,7},{7,6},{8,9},{9,8},{10,11... | collective-permute-start | bytes 2359304 | tf_op jit(solution)/shard_map/ppermute | solution.py:210
  21.9 25.4 %collective-permute-start.2 = (bf16[128,3072]{1,0:T(8,128)(2,1)}, bf16[128,3072]{1,0:T(8,128)(2,1)}, u32[]{:S(2)}, u32[]{:S(2)}) collective-permute-start(bf16[128,3072]{1,0:T(8,128)(2,1)} %bitcast.11), channel_id=1, source_target_pairs={{0,4},{1,5},{2,6},{3,7},{4,0},{5,1},{6,2},{7,3},{8,12},{9,13},{10,... | collective-permute-start | bytes 2359304 | tf_op jit(solution)/shard_map/ppermute | solution.py:210
  23.8 38.1 %collective-permute-start.1 = (bf16[128,3072]{1,0:T(8,128)(2,1)}, bf16[128,3072]{1,0:T(8,128)(2,1)S(1)}, u32[]{:S(2)}, u32[]{:S(2)}) collective-permute-start(bf16[128,3072]{1,0:T(8,128)(2,1)} %bitcast.12), channel_id=1, source_target_pairs={{0,2},{1,3},{2,4},{3,5},{4,6},{5,7},{6,0},{7,1},{8,10},{9,11},{10,... | collective-permute-start | bytes 2359304 | tf_op jit(solution)/shard_map/ppermute | solution.py:210
  25.8 37.1 %collective-permute-start = (bf16[128,3072]{1,0:T(8,128)(2,1)}, bf16[128,3072]{1,0:T(8,128)(2,1)S(1)}, u32[]{:S(2)}, u32[]{:S(2)}) collective-permute-start(bf16[128,3072]{1,0:T(8,128)(2,1)} %bitcast.13), channel_id=1, source_target_pairs={{0,6},{1,7},{2,0},{3,1},{4,2},{5,3},{6,4},{7,5},{8,14},{9,15},{10,... | collective-permute-start | bytes 2359304 | tf_op jit(solution)/shard_map/ppermute | solution.py:210
  40.3 38.6 %collective-permute-start.5 = (bf16[128,3072]{1,0:T(8,128)(2,1)}, bf16[128,3072]{1,0:T(8,128)(2,1)}, u32[]{:S(2)}, u32[]{:S(2)}) collective-permute-start(bf16[128,3072]{1,0:T(8,128)(2,1)} %collective-permute-done.3.refs_0_), channel_id=1, source_target_pairs={{0,2},{1,3},{2,4},{3,5},{4,6},{5,7},{6,0},{7,1},{8,10},{9,11},{10,... | collective-permute-start | bytes 2359304 | tf_op jit(solution)/shard_map/ppermute | solution.py:210
  42.2 36.7 %collective-permute-start.4 = (bf16[128,3072]{1,0:T(8,128)(2,1)}, bf16[128,3072]{1,0:T(8,128)(2,1)}, u32[]{:S(2)}, u32[]{:S(2)}) collective-permute-start(bf16[128,3072]{1,0:T(8,128)(2,1)} %collective-permute-done.3.refs_0_), channel_id=1, source_target_pairs={{0,6},{1,7},{2,0},{3,1},{4,2},{5,3},{6,4},{7,5},{8,14},{9,15},{10,... | collective-permute-start | bytes 2359304 | tf_op jit(solution)/shard_map/ppermute | solution.py:210
  47.3 31.5 %collective-permute-start.6 = (bf16[128,3072]{1,0:T(8,128)(2,1)}, bf16[128,3072]{1,0:T(8,128)(2,1)}, u32[]{:S(2)}, u32[]{:S(2)}) collective-permute-start(bf16[128,3072]{1,0:T(8,128)(2,1)} %collective-permute-done.2.refs_3_), channel_id=1, source_target_pairs={{0,1},{1,0},{2,3},{3,2},{4,5},{5,4},{6,7},{7,6},{8,9},{9,8},{10,11... | collective-permute-start | bytes 2359304 | tf_op jit(solution)/shard_map/ppermute | solution.py:210
  62.0 0.9 copy-start.3
  62.9 1.0 copy-start.5
  63.9 1.1 copy-start.2
  65.0 1.1 copy-start.4
  66.1 1.1 copy-start.6
  81.3 1.7 %copy-start = (bf16[512,3072]{1,0:T(8,128)(2,1)}, bf16[512,3072]{1,0:T(8,128)(2,1)S(1)}, u32[]{:S(2)}) copy-start(bf16[512,3072]{1,0:T(8,128)(2,1)S(1)} %shard_map.47.refs_2_.refs_3_) | copy-start | bytes 9437188
  96.6 2.9 %copy-start.1 = (bf16[512,3072]{1,0:T(8,128)(2,1)S(1)}, bf16[512,3072]{1,0:T(8,128)(2,1)}, u32[]{:S(2)}) copy-start(bf16[512,3072]{1,0:T(8,128)(2,1)} %copy-done) | copy-start | bytes 9437188
  101.3 23.9 %collective-permute-start.10 = (bf16[1024,256]{1,0:T(8,128)(2,1)S(1)}, bf16[1024,256]{1,0:T(8,128)(2,1)S(1)}, u32[]{:S(2)}, u32[]{:S(2)}) collective-permute-start(bf16[1024,256]{1,0:T(8,128)(2,1)S(1)} %shard_map.48.refs_2_), channel_id=1, source_target_pairs={{8,0},{16,8},{24,16},{32,24},{40,32},{48,40},{56,48},{64,56},{72,6... | collective-permute-start | bytes 1572872 | tf_op jit(solution)/shard_map/ppermute | solution.py:241
  103.2 21.9 %collective-permute-start.9 = (bf16[1024,256]{1,0:T(8,128)(2,1)S(1)}, bf16[1024,256]{1,0:T(8,128)(2,1)S(1)}, u32[]{:S(2)}, u32[]{:S(2)}) collective-permute-start(bf16[1024,256]{1,0:T(8,128)(2,1)S(1)} %shard_map.48.refs_2_), channel_id=1, source_target_pairs={{0,8},{8,16},{16,24},{24,32},{32,40},{40,48},{48,56},{56,64},{64,7... | collective-permute-start | bytes 1572872 | tf_op jit(solution)/shard_map/ppermute | solution.py:240
  107.4 5.6 %slice-start = ((bf16[3072,640]{1,0:T(8,128)(2,1)}), bf16[3072,128]{1,0:T(8,128)(2,1)S(1)}, s32[]{:S(2)}) async-start(bf16[3072,640]{1,0:T(8,128)(2,1)} %all-gather.2.cloned.1.call-done), calls=%async_computation.1 | async-start | bytes 1572864 | tf_op jit(solution)/shard_map/slice | solution.py:242
  107.4 20.7 %collective-permute-start.8 = (bf16[1024,256]{1,0:T(8,128)(2,1)S(1)}, bf16[1024,256]{1,0:T(8,128)(2,1)S(1)}, u32[]{:S(2)}, u32[]{:S(2)}) collective-permute-start(bf16[1024,256]{1,0:T(8,128)(2,1)S(1)} %shard_map.49.refs_3_), channel_id=1, source_target_pairs={{8,0},{16,8},{24,16},{32,24},{40,32},{48,40},{56,48},{64,56},{72,6... | collective-permute-start | bytes 1572872 | tf_op jit(solution)/shard_map/ppermute | solution.py:241
  110.7 18.4 %collective-permute-start.7 = (bf16[1024,256]{1,0:T(8,128)(2,1)S(1)}, bf16[1024,256]{1,0:T(8,128)(2,1)S(1)}, u32[]{:S(2)}, u32[]{:S(2)}) collective-permute-start(bf16[1024,256]{1,0:T(8,128)(2,1)S(1)} %shard_map.49.refs_3_), channel_id=1, source_target_pairs={{0,8},{8,16},{16,24},{24,32},{32,40},{40,48},{48,56},{56,64},{64,7... | collective-permute-start | bytes 1572872 | tf_op jit(solution)/shard_map/ppermute | solution.py:240
Sparse Core Ops, SparseCore 0:
  14.2 82.3 all-gather.1
